TPU v7x, 256 devices: a whole 4x4x8 slice. The times are simulated.
256 devices in a mesh: resp: 8 (over x, y_hi), blk: 32 (over z, y_lo, core).
Axes of the slice: x: 4, y: 4 (y_hi: 2, y_lo: 2; y = y_hi * 2 + y_lo), z: 8, core: 2. Of those that a mesh axis runs over, the one named last changes fastest.
Arguments:
- response_query: bfloat16 [8, 4096, 1792], P('resp', 'blk'), may hold values from -8 to 8
- response_key: bfloat16 [8, 4096, 256], P('resp', 'blk'), may hold values from -6 to 6
- response_value: bfloat16 [8, 4096, 256], P('resp', 'blk'), may hold values from -6 to 6
- shared_prompt_key: bfloat16 [2048, 256], P('blk'), may hold values from -8 to 8
- shared_prompt_value: bfloat16 [2048, 256], P('blk'), may hold values from -6 to 6
- grad_out: bfloat16 [8, 4096, 1792], P('resp', 'blk'), may hold values from -48 to 48
- lengths: int32 [8], P('resp'), may hold values from 128 to 4096, as said below
Outputs:
- grad_q: bfloat16 [8, 4096, 1792], P('resp', 'blk')
- grad_k_resp: bfloat16 [8, 4096, 256], P('resp', 'blk')
- grad_v_resp: bfloat16 [8, 4096, 256], P('resp', 'blk')
- prompt_key_gradient: bfloat16 [2048, 256], P('blk')
- prompt_value_gradient: bfloat16 [2048, 256], P('blk')
Inputs may be any that keep to these rules, and one draw needn't show every extreme that they name: `lengths`: multiples of 128.
All inputs are finite; a program needn't handle non-finite values.
Results may differ from a plain program's by a relative error of at most 0.014.
Values may be sent and summed in bfloat16 or wider, within the bound.
A program may use at most 64 MiB of HBM per device.

v0:
```python
import jax
import jax.numpy as jnp
from jax import lax
from jax.sharding import PartitionSpec as P

QUERY_HEADS = 14
KEY_VALUE_HEADS = 2
HEAD_WIDTH = 128


def head_logits(query_rows, key_block, logit_scale):
    return (
        jnp.einsum("tgjd,kgd->gjtk", query_rows, key_block, preferred_element_type=jnp.float32)
        * logit_scale
    )


def shards(
    response_query,
    response_key,
    response_value,
    shared_prompt_key,
    shared_prompt_value,
    grad_out,
    lengths,
):
    token_rows = response_query.shape[1]
    prompt_rows = shared_prompt_key.shape[0]
    kv_width = shared_prompt_key.shape[1]
    group_width = QUERY_HEADS // KEY_VALUE_HEADS
    logit_scale = HEAD_WIDTH ** (-0.5)
    my_index = lax.axis_index("blk")
    first_row = my_index * token_rows
    resp_length = lengths[0]
    positions = first_row + jnp.arange(token_rows, dtype=jnp.int32)
    gradient_rows = jnp.where(
        (positions < resp_length)[:, None], grad_out[0], jnp.zeros_like(grad_out[0])
    )
    query_rows = response_query[0].reshape(token_rows, KEY_VALUE_HEADS, group_width, HEAD_WIDTH)
    gradient_heads = gradient_rows.reshape(token_rows, KEY_VALUE_HEADS, group_width, HEAD_WIDTH)
    all_pkey, all_pvalue, all_rkey, all_rvalue = (
        lax.all_gather(shared_prompt_key, "blk", axis=0, tiled=True),
        lax.all_gather(shared_prompt_value, "blk", axis=0, tiled=True),
        lax.all_gather(response_key[0], "blk", axis=0, tiled=True),
        lax.all_gather(response_value[0], "blk", axis=0, tiled=True),
    )
    prompt_len = all_pkey.shape[0]
    resp_len = all_rkey.shape[0]
    prompt_step = min(512, prompt_len)
    resp_step = min(512, resp_len)
    dev_live = first_row < resp_length
    reach_end = jnp.minimum(first_row + token_rows, resp_length)

    def take(source, block_start, block_length):
        return lax.dynamic_slice_in_dim(source, block_start, block_length, 0).reshape(
            block_length, KEY_VALUE_HEADS, HEAD_WIDTH
        )

    def mask_for(block_start, block_length):
        return (block_start + jnp.arange(block_length, dtype=jnp.int32))[None, :] <= positions[
            :, None
        ]

    def block_stats(running, key_block, value_block, visible):
        row_top, row_total, weighted = running
        logits = head_logits(query_rows, key_block, logit_scale)
        if visible is not None:
            logits = jnp.where(visible, logits, -jnp.inf)
        grad_prob = jnp.einsum(
            "tgjd,kgd->gjtk", gradient_heads, value_block, preferred_element_type=jnp.float32
        )
        new_top = jnp.maximum(row_top, jnp.max(logits, axis=-1))
        scaled = jnp.exp(logits - new_top[..., None])
        rescale = jnp.exp(row_top - new_top)
        return (
            new_top,
            row_total * rescale + jnp.sum(scaled, axis=-1),
            weighted * rescale + jnp.sum(scaled * grad_prob, axis=-1),
        )

    statistic_shape = (KEY_VALUE_HEADS, group_width, token_rows)
    initial = (
        jnp.full(statistic_shape, -jnp.inf, jnp.float32),
        jnp.zeros(statistic_shape, jnp.float32),
        jnp.zeros(statistic_shape, jnp.float32),
    )

    def prompt_stats(block_index, running):
        block_start = block_index * prompt_step
        return block_stats(
            running,
            take(all_pkey, block_start, prompt_step),
            take(all_pvalue, block_start, prompt_step),
            None,
        )

    def resp_stats(block_index, running):
        block_start = block_index * resp_step
        key_block = take(all_rkey, block_start, resp_step)
        value_block = take(all_rvalue, block_start, resp_step)
        visible = mask_for(block_start, resp_step)
        return lax.cond(
            dev_live & (block_start < reach_end),
            lambda current: block_stats(current, key_block, value_block, visible),
            lambda current: current,
            running,
        )

    running = lax.fori_loop(0, prompt_len // prompt_step, prompt_stats, initial)
    running = lax.fori_loop(0, resp_len // resp_step, resp_stats, running)
    row_top, row_total, weighted = running
    log_total = (row_top + jnp.log(row_total))[..., None]
    grad_dot = (weighted / row_total)[..., None]

    def block_grads(key_block, value_block, visible):
        logits = head_logits(query_rows, key_block, logit_scale)
        if visible is not None:
            logits = jnp.where(visible, logits, -jnp.inf)
        weights = jnp.exp(logits - log_total)
        grad_prob = jnp.einsum(
            "tgjd,kgd->gjtk", gradient_heads, value_block, preferred_element_type=jnp.float32
        )
        grad_logit = (weights * (grad_prob - grad_dot)).astype(jnp.bfloat16)
        weights_low = weights.astype(jnp.bfloat16)
        query_add = jnp.einsum(
            "gjtk,kgd->tgjd", grad_logit, key_block, preferred_element_type=jnp.float32
        )
        key_add = (
            jnp.einsum("gjtk,tgjd->kgd", grad_logit, query_rows, preferred_element_type=jnp.float32)
            * logit_scale
        )
        value_add = jnp.einsum(
            "gjtk,tgjd->kgd", weights_low, gradient_heads, preferred_element_type=jnp.float32
        )
        return (query_add, key_add.reshape(-1, kv_width), value_add.reshape(-1, kv_width))

    query_initial = jnp.zeros((token_rows, KEY_VALUE_HEADS, group_width, HEAD_WIDTH), jnp.float32)

    def prompt_grads(block_index, running):
        query_sum, key_sum, value_sum = running
        block_start = block_index * prompt_step
        query_add, key_add, value_add = block_grads(
            take(all_pkey, block_start, prompt_step),
            take(all_pvalue, block_start, prompt_step),
            None,
        )
        key_sum = lax.dynamic_update_slice_in_dim(key_sum, key_add, block_start, 0)
        value_sum = lax.dynamic_update_slice_in_dim(value_sum, value_add, block_start, 0)
        return (query_sum + query_add, key_sum, value_sum)

    prompt_zero = jnp.zeros((prompt_len, kv_width), jnp.float32)
    query_sum, prompt_key_grads, prompt_value_grads = lax.fori_loop(
        0, prompt_len // prompt_step, prompt_grads, (query_initial, prompt_zero, prompt_zero)
    )

    def resp_grads(block_index, running):
        query_sum, key_sum, value_sum = running
        block_start = block_index * resp_step
        key_block = take(all_rkey, block_start, resp_step)
        value_block = take(all_rvalue, block_start, resp_step)
        visible = mask_for(block_start, resp_step)

        def compute(current):
            return block_grads(key_block, value_block, visible)

        def nothing(current):
            empty_rows = jnp.zeros((resp_step, kv_width), jnp.float32)
            return (query_initial, empty_rows, empty_rows)

        query_add, key_add, value_add = lax.cond(
            dev_live & (block_start < reach_end), compute, nothing, 0
        )
        key_sum = lax.dynamic_update_slice_in_dim(key_sum, key_add, block_start, 0)
        value_sum = lax.dynamic_update_slice_in_dim(value_sum, value_add, block_start, 0)
        return (query_sum + query_add, key_sum, value_sum)

    resp_zero = jnp.zeros((resp_len, kv_width), jnp.float32)
    query_sum, resp_kgrad, resp_vgrad = lax.fori_loop(
        0, resp_len // resp_step, resp_grads, (query_sum, resp_zero, resp_zero)
    )
    grad_q = (
        (query_sum * logit_scale)
        .reshape(token_rows, QUERY_HEADS * HEAD_WIDTH)
        .astype(jnp.bfloat16)[None]
    )
    response_key_gradient, response_value_gradient = (
        lax.psum_scatter(resp_kgrad, "blk", scatter_dimension=0, tiled=True),
        lax.psum_scatter(resp_vgrad, "blk", scatter_dimension=0, tiled=True),
    )
    grad_k_resp = response_key_gradient.astype(jnp.bfloat16)[None]
    grad_v_resp = response_value_gradient.astype(jnp.bfloat16)[None]
    total_k, total_v = lax.psum((prompt_key_grads, prompt_value_grads), ("resp", "blk"))
    offset = my_index * prompt_rows
    block_k = lax.dynamic_slice_in_dim(total_k, offset, prompt_rows, 0)
    block_v = lax.dynamic_slice_in_dim(total_v, offset, prompt_rows, 0)
    prompt_key_gradient = block_k.astype(jnp.bfloat16)
    prompt_value_gradient = block_v.astype(jnp.bfloat16)
    return (grad_q, grad_k_resp, grad_v_resp, prompt_key_gradient, prompt_value_gradient)


def solution(mesh):
    in_specs = (
        P("resp", "blk", None),
        P("resp", "blk", None),
        P("resp", "blk", None),
        P("blk", None),
        P("blk", None),
        P("resp", "blk", None),
        P("resp"),
    )
    out_specs = (
        P("resp", "blk", None),
        P("resp", "blk", None),
        P("resp", "blk", None),
        P("blk", None),
        P("blk", None),
    )
    return jax.shard_map(shards, mesh=mesh, in_specs=in_specs, out_specs=out_specs, check_vma=False)
```

profile of v0, /device:TPU:1, one launch (start us, length us, event | category | flops | bytes accessed | tf_op | source)
XLA Modules:
  0.0 694.8 jit_solution(16205408074068650498)
XLA Ops:
  8.7 1.6 copy.96
  10.3 1.6 copy.97
  14.2 1.3 copy.91
  15.8 61.9 %all-gather.7.cloned.1.call-done = bf16[2048,256]{1,0:T(8,128)(2,1)} async-done(((bf16[64,256]{1,0:T(8,128)(2,1)}), bf16[2048,256]{1,0:T(8,128)(2,1)}) %all-gather.7.cloned.1.call-update) | async-done | bytes 1048592 | tf_op jit(solution)/shard_map/all_gather | solution.py:42
  77.7 2.3 copy.100
  80.0 62.9 %all-gather.9.cloned.1.call-done = bf16[2048,256]{1,0:T(8,128)(2,1)} async-done(((bf16[64,256]{1,0:T(8,128)(2,1)}), bf16[2048,256]{1,0:T(8,128)(2,1)}) %all-gather.9.cloned.1.call-update) | async-done | bytes 1048592 | tf_op jit(solution)/shard_map/all_gather | solution.py:43
  142.9 2.3 copy.94
  145.1 14.2 %while.74 = (s32[]{:T(128)}, f32[2,7,128]{2,1,0:T(8,128)S(1)}, f32[2,7,128]{2,1,0:T(8,128)S(1)}, f32[2,7,128]{2,1,0:T(8,128)S(1)}, bf16[2048,256]{0,1:T(8,128)(2...) while((s32[]{:T(128)}, f32[2,7,128]{2,1,0:T(8,128)S(1)}, ...), condition=%wide.region_4.5_spmd.clone, body=%wide.region_0.4_spmd.clone.sunk | while | flops 478032128 | bytes 13629626 | solution.py:109
  159.3 51.6 %all-gather.11.cloned.1.call-done = bf16[1,4096,256]{1,2,0:T(8,128)(2,1)} async-done(((bf16[1,128,256]{1,2,0:T(8,128)(2,1)}), bf16[1,4096,256]{1,2,0:T(8,128)(2,1)}) %all-gather.11.cloned.1.call-update) | async-done | bytes 2097168 | tf_op jit(solution)/shard_map/all_gather | solution.py:44
  210.9 66.3 %all-gather.13.cloned.1.call-done = bf16[1,4096,256]{1,2,0:T(8,128)(2,1)} async-done(((bf16[1,128,256]{1,2,0:T(8,128)(2,1)}), bf16[1,4096,256]{1,2,0:T(8,128)(2,1)}) %all-gather.13.cloned.1.call-update) | async-done | bytes 2097168 | tf_op jit(solution)/shard_map/all_gather | solution.py:45
  277.2 4.6 while.72
  277.2 4.0 conditional.6
  281.8 1.4 broadcast_in_dim.81.clone2
  283.2 1.5 broadcast_in_dim.81.clone
  284.7 51.0 %while.75 = (s32[]{:T(128)}, f32[128,2,7,128]{0,3,2,1:T(8,128)}, f32[2048,256]{1,0:T(8,128)}, f32[2048,256]{1,0:T(8,128)}, bf16[2048,256]{0,1:T(8,128)(2,1)}, /*...) while((s32[]{:T(128)}, f32[128,2,7,128]{0,3,2,1:T(8,128)}, ...), condition=%wide.region_13.14_spmd.clone, body=%wide.region_12.13_spmd.clone.sunk | while | flops 1182334976 | bytes 27284688 | solution.py:152
  287.3 1.6 fusion.104
  291.3 1.5 fusion.105
  292.8 1.4 fusion.103
  299.2 1.6 fusion.104
  303.1 1.5 fusion.105
  304.7 2.6 fusion.103
  312.2 1.6 fusion.104
  316.2 1.5 fusion.105
  317.7 2.6 fusion.103
  325.3 1.6 fusion.104
  329.2 1.5 fusion.105
  330.8 2.6 fusion.103
  335.7 2.4 copy.102
  338.1 2.2 broadcast_in_dim.87.clone2
  340.3 2.2 broadcast_in_dim.87.clone
  342.5 36.6 %while.73 = (s32[]{:T(128)}, f32[128,2,7,128]{3,0,2,1:T(8,128)}, f32[4096,256]{1,0:T(8,128)}, f32[4096,256]{1,0:T(8,128)}, s32[]{:T(128)}, /*index=5*/pred[]{:T(...) while((s32[]{:T(128)}, f32[128,2,7,128]{3,0,2,1:T(8,128)}, ...), condition=%wide.region_17.18_spmd.clone, body=%wide.region_14.17_spmd.clone.sunk | while | flops 1184006784 | bytes 29327192 | solution.py:178
  342.6 5.8 conditional.7
  345.5 1.3 fusion.8
  348.4 2.2 add.268
  352.2 2.2 add.268
  356.1 2.2 add.268
  360.0 2.2 add.268
  363.9 2.2 add.268
  367.8 2.2 add.268
  371.6 2.2 add.268
  375.5 2.2 add.268
  380.4 1.3 copy.103
  381.7 1.3 multiply_convert_fusion
  384.0 197.9 %all-reduce.2 = (bf16[2048,256]{1,0:T(8,128)(2,1)}, bf16[2048,256]{1,0:T(8,128)(2,1)}) all-reduce(f32[2048,256]{1,0:T(8,128)} %get-tuple-element.958, f32[2048,256]{1,0:T(8,128)S(1)} %copy-done.1), channel_id=1, replica_groups=mesh['resp'=8,'blk'=32] {'resp','blk'}, use_global_device_ids=true, to_apply=%region_20.21 | all-reduce | flops 1048576 | bytes 6291456 | tf_op jit(solution)/shard_map/psum | solution.py:192
  581.9 1.4 dynamic-slice_convert_fusion
  583.3 1.5 convert_bitcast_fusion
  584.8 101.6 %reduce-scatter.3.cloned.1.call-done = f32[128,256]{1,0:T(8,128)} async-done(((f32[4096,256]{1,0:T(8,128)}), f32[128,256]{1,0:T(8,128)}) %reduce-scatter.3.cloned.1.call-update) | async-done | bytes 131088 | tf_op jit(solution)/shard_map/reduce_scatter | solution.py:187
  686.4 1.5 convert_bitcast_fusion.1
  (193 shorter events, 71.4 us)
Async XLA Ops:
  7.2 70.5 %all-gather.7.cloned.1.call-start = ((), (), s32[]{:S(2)}) async-start(), calls=%async_computation.2 | async-start | bytes 1081344 | tf_op jit(solution)/shard_map/all_gather | solution.py:42
  7.9 135.0 %all-gather.9.cloned.1.call-start = ((), (), s32[]{:S(2)}) async-start(), calls=%async_computation.3 | async-start | bytes 1081344 | tf_op jit(solution)/shard_map/all_gather | solution.py:43
  8.6 202.2 %all-gather.11.cloned.1.call-start = ((), (), s32[]{:S(2)}) async-start(), calls=%async_computation.6 | async-start | bytes 2162688 | tf_op jit(solution)/shard_map/all_gather | solution.py:44
  10.3 266.9 %all-gather.13.cloned.1.call-start = ((), (), s32[]{:S(2)}) async-start(), calls=%async_computation.7 | async-start | bytes 2162688 | tf_op jit(solution)/shard_map/all_gather | solution.py:45
  11.9 571.3 %reduce-scatter.5.cloned.1.call-start = ((), (), s32[]{:S(2)}) async-start(), calls=%async_computation.5 | async-start | bytes 4325376 | tf_op jit(solution)/shard_map/reduce_scatter | solution.py:188
  379.2 1.2 copy-start
  379.2 307.2 %reduce-scatter.3.cloned.1.call-start = ((), (), s32[]{:S(2)}) async-start(), calls=%async_computation.4 | async-start | bytes 4325376 | tf_op jit(solution)/shard_map/reduce_scatter | solution.py:187
  379.3 4.7 copy-start.1
Sparse Core Ops, SparseCore 0:
  9.9 67.7 all-gather.6
  79.6 63.2 all-gather.8
  145.2 65.6 all-gather.10
  213.1 64.0 all-gather.12
  379.3 183.7 reduce-scatter.4
  565.5 120.8 reduce-scatter.2
where the time goes:
time: 700 us; the launch traced here: 695 us
  waiting for transfers between devices  346 us (49%)
  blocking collectives  198 us (28%)
  local copies, waits for them, and re-layouts  66.1 us (9%)
  matrix products  42.5 us (6%)
  other arithmetic  25.7 us (4%)
  between operations  14.9 us (2%)
    psum x1, blocking collectives, shards(): lax.psum((prompt_key_grads, prompt_value_grads), ('resp', 'blk'))  198 us
    reduce_scatter x1, waiting for transfers between devices, shards(): lax.psum_scatter(resp_kgrad, 'blk', scatter_dimension=0, tiled=True)  102 us
    all_gather x1, waiting for transfers between devices, shards(): lax.all_gather(response_value[0], 'blk', axis=0, tiled=True)  66.3 us
    all_gather x1, waiting for transfers between devices, shards(): lax.all_gather(shared_prompt_value, 'blk', axis=0, tiled=True)  62.9 us
    all_gather x1, waiting for transfers between devices, shards(): lax.all_gather(shared_prompt_key, 'blk', axis=0, tiled=True)  61.9 us
    all_gather x1, waiting for transfers between devices, shards(): lax.all_gather(response_key[0], 'blk', axis=0, tiled=True)  51.6 us
    add x8, other arithmetic, resp_grads(): return (query_sum + query_add, key_sum, value_sum)  17.7 us
    unnamed x14, local copies, waits for them, and re-layouts  14.7 us
  transfers between devices with their start and end apart: 6, of which 5 were waited for; matrix products, arithmetic and copies ran while one was open for 5% of the time, Pallas kernels for 0%

commit v1 on v0

v1 whole, which is shorter than its diff:
```python
import functools

import jax
import jax.numpy as jnp
from jax import lax
from jax.experimental import pallas as pl
from jax.experimental.pallas import tpu as pltpu
from jax.sharding import PartitionSpec as P

HEADS = 7
D = 128
RESP = 4096
PROMPT = 2048
SCALE = D**-0.5
LOG2E = 1.4426950408889634
KC = 512
f32, bf16 = jnp.float32, jnp.bfloat16
MESH = pl.DeviceIdType.MESH
ANY = pl.BlockSpec(memory_space=pl.ANY)
VMEM = pl.BlockSpec(memory_space=pltpu.VMEM)
SMEM = pl.BlockSpec(memory_space=pltpu.SMEM)


def dot(a, b):
    return jnp.dot(a, b, preferred_element_type=f32)


def place():
    r, b = lax.axis_index("resp"), lax.axis_index("blk")
    z, y, c = b // 4, lax.rem(b // 2, 2), lax.rem(b, 2)
    return r, b, z, y, c


def aligned(start, size):
    return pl.ds(pl.multiple_of(start, size), size)


def mod8(value):
    return lax.rem(value + 16, 8)


def barrier(peers):
    sem = pltpu.get_barrier_semaphore()
    for peer in peers:
        pl.semaphore_signal(sem, inc=1, device_id=peer, device_id_type=MESH)
    pl.semaphore_wait(sem, len(peers))


def gather_kernel(
    q, g, rk, rv, pk, pv, qh, gh, kr, vr, kp, vp,
    own_sem, sib_s, sib_r, ky_s, ky_r, kz_s, kz_r, vz_s, vz_r, vy_s, vy_r,
):
    r, b, z, y, c = place()
    p = z * 2 + y
    sib = (r, b + 1 - 2 * c)
    yn = (r, b + 2 - 4 * y)
    zr = (r, lax.rem(b + 4, 32))
    zl = (r, lax.rem(b + 28, 32))
    barrier((sib, yn, zr, zl))

    def swap(i, src, dst, start, rows, width):
        mine = pltpu.make_async_copy(
            src.at[:, aligned(c * width, width)], dst.at[aligned(start, rows), :], own_sem.at[i]
        )
        theirs = pltpu.make_async_remote_copy(
            src_ref=src.at[:, aligned((1 - c) * width, width)],
            dst_ref=dst.at[aligned(start, rows), :],
            send_sem=sib_s.at[i],
            recv_sem=sib_r.at[i],
            device_id=sib,
            device_id_type=MESH,
        )
        mine.start()
        theirs.start()
        return mine, theirs

    first = p * 256 + c * 128
    swaps = [
        swap(0, pk, kp, p * 128 + c * 64, 64, 128),
        swap(1, pv, vp, p * 128 + c * 64, 64, 128),
        swap(2, rk, kr, first, 128, 128),
        swap(3, rv, vr, first, 128, 128),
        swap(4, q, qh, c * 128, 128, 896),
        swap(5, g, gh, c * 128, 128, 896),
    ]
    for mine, theirs in swaps[:4]:
        mine.wait()
        theirs.wait_recv()

    sent = []

    def send(ref, start, rows, to, s_sem, r_sem):
        copy = pltpu.make_async_remote_copy(
            src_ref=ref.at[aligned(start, rows), :],
            dst_ref=ref.at[aligned(start, rows), :],
            send_sem=s_sem,
            recv_sem=r_sem,
            device_id=to,
            device_id_type=MESH,
        )
        copy.start()
        sent.append(copy)
        return copy

    arrays = ((0, kp, vp, 128), (1, kr, vr, 256))
    pending_ky, pending_kz, pending_vz, pending_vy = [], [], [], []

    def start_ky():
        for i, kx, _, n in arrays:
            pending_ky.append(send(kx, p * n, n, yn, ky_s.at[i], ky_r.at[i]))

    def start_vz(step):
        for i, _, vx, n in arrays:
            for way, to in ((0, zr), (1, zl)):
                t = mod8(z - step + 1) if way == 0 else mod8(z + step - 1)
                start, rows = (t * 2 + y) * n, n
                if step == 4:
                    rows = n // 2
                    start = start + way * rows
                k = i * 8 + way * 4 + step - 1
                pending_vz.append(send(vx, start, rows, to, vz_s.at[k], vz_r.at[k]))

    def start_vy(slots):
        for i, _, vx, n in arrays:
            for slot, t in slots:
                k = i * 8 + slot
                pending_vy.append(send(vx, (t * 2 + y) * n, n, yn, vy_s.at[k], vy_r.at[k]))

    def start_kz(step):
        for i, kx, _, n in arrays:
            for way, to in ((0, zr), (1, zl)):
                t = mod8(z - step + 1) if way == 0 else mod8(z + step - 1)
                start, rows = t * 2 * n, 2 * n
                if step == 4:
                    rows = n
                    start = start + way * rows
                k = i * 8 + way * 4 + step - 1
                pending_kz.append(send(kx, start, rows, to, kz_s.at[k], kz_r.at[k]))

    def drain(pending):
        for copy in pending:
            copy.wait_recv()
        pending.clear()

    start_ky()
    start_vz(1)
    start_vy([(0, z)])
    drain(pending_ky)
    start_kz(1)
    for step in range(2, 5):
        drain(pending_vz)
        start_vz(step)
        start_vy([(step - 1, mod8(z - step + 1)), (step + 3, mod8(z + step - 1))])
        drain(pending_kz)
        start_kz(step)
    drain(pending_vz)
    start_vy([(4, mod8(z + 4))])
    drain(pending_kz)
    drain(pending_vy)
    for mine, theirs in swaps[4:]:
        mine.wait()
        theirs.wait_recv()
    for _, theirs in swaps:
        theirs.wait_send()
    for copy in sent:
        copy.wait_send()


def compute_kernel(
    length, q, g_in, kr, vr, kp, vp, dq, dkr, dvr, dkp, dvp,
    g, kt, qt, gt, pb, dpb, mb, dk, dv,
):
    _, _, z, y, c = place()
    chip = z * 2 + y
    for i in range(PROMPT // 512):
        kt[:, i * 512 : (i + 1) * 512] = kp[i * 512 : (i + 1) * 512, :].T

    @pl.loop(0, RESP // 512)
    def _(i):
        kt[:, aligned(PROMPT + i * 512, 512)] = kr[aligned(i * 512, 512), :].T

    row = lax.broadcasted_iota(jnp.int32, (256, 896), 0) + chip * 256
    g[...] = jnp.where(row < length[0], g_in[...].astype(f32), 0.0).astype(bf16)
    dk[...] = jnp.zeros_like(dk)
    dv[...] = jnp.zeros_like(dv)
    n_resp = chip // 2

    def head(j, _):
        cols = aligned(j * 128, 128)
        qj = q[:, cols]
        gj = g[:, cols]
        qt[...] = qj.T
        gt[...] = gj.T

        def stats(k_src, v_src, start, base, carry, masked):
            m, l, d = carry
            s = dot(k_src[aligned(start, KC), :], qt[...]) * (SCALE * LOG2E)
            dp = dot(v_src[aligned(start, KC), :], gt[...])
            if masked:
                key = lax.broadcasted_iota(jnp.int32, s.shape, 0) + start
                pos = lax.broadcasted_iota(jnp.int32, s.shape, 1) + chip * 256
                s = jnp.where(key <= pos, s, -jnp.inf)
            top = jnp.maximum(m, jnp.max(s, axis=0, keepdims=True))
            back = jnp.exp2(m - top)
            w = jnp.exp2(s - top)
            l = l * back + jnp.sum(w, axis=0, keepdims=True)
            d = d * back + jnp.sum(w * dp, axis=0, keepdims=True)
            pb[aligned(base, KC), :] = w.astype(bf16)
            dpb[aligned(base, KC), :] = dp
            mb[base // KC] = jnp.broadcast_to(top, (8, 256))
            return top, l, d

        carry = (
            jnp.full((1, 256), -jnp.inf, f32),
            jnp.zeros((1, 256), f32),
            jnp.zeros((1, 256), f32),
        )
        carry = lax.fori_loop(
            0, PROMPT // KC, lambda i, x: stats(kp, vp, i * KC, i * KC, x, False), carry, unroll=2
        )
        carry = lax.fori_loop(
            0, n_resp, lambda i, x: stats(kr, vr, i * KC, PROMPT + i * KC, x, False), carry
        )
        m, l, d = stats(kr, vr, n_resp * KC, PROMPT + n_resp * KC, carry, True)
        inv = 1.0 / l
        d = d * inv

        def grads(base, acc):
            r = jnp.exp2(mb[base // KC][0:1] - m) * inv
            w = pb[aligned(base, KC), :].astype(f32) * r
            ds = (w * (dpb[aligned(base, KC), :] - d)).astype(bf16)
            dk[aligned(base, KC), :] += dot(ds, qj)
            dv[aligned(base, KC), :] += dot(w.astype(bf16), gj)
            return acc + dot(kt[:, aligned(base, KC)], ds)

        acc = lax.fori_loop(
            0, PROMPT // KC, lambda i, x: grads(i * KC, x), jnp.zeros((128, 256), f32), unroll=2
        )
        acc = lax.fori_loop(0, n_resp + 1, lambda i, x: grads(PROMPT + i * KC, x), acc)
        dq[:, cols] = (acc.T * SCALE).astype(bf16)
        return 0

    lax.fori_loop(0, HEADS, head, 0)
    dkp[...] = (dk[:PROMPT, :] * SCALE).astype(bf16)
    dvp[...] = dv[:PROMPT, :].astype(bf16)
    dkr[...] = (dk[PROMPT:, :] * SCALE).astype(bf16)
    dvr[...] = dv[PROMPT:, :].astype(bf16)


def reduce_kernel(
    dq, dkr, dvr, dkp, dvp, gq, gk, gv, pkg, pvg,
    k_out, k_in, v_out, v_in, v_y, ky_out, ky_in, fin, x_in, xs, yz_in, g_out,
    q_sem, kz_s, kz_r, vz_s, vz_r, vy_s, vy_r, ky_s, ky_r, f_sem, x_s, x_r, yz_s, yz_r, g_s, g_r,
):
    r, b, z, y, c = place()
    x, y_hi = r // 2, lax.rem(r, 2)
    p = z * 2 + y
    sib = (r, b + 1 - 2 * c)
    yn = (r, b + 2 - 4 * y)
    zr = (r, lax.rem(b + 4, 32))
    zl = (r, lax.rem(b + 28, 32))

    def yz_peer(o):
        yh = lax.rem(y_hi + o // 16, 2)
        zz = lax.rem(z + lax.rem(o // 2, 8), 8)
        yl = lax.rem(y + lax.rem(o, 2), 2)
        return yh, zz, yl

    sem = pltpu.get_barrier_semaphore()

    @pl.loop(1, 32)
    def _(o):
        yh, zz, yl = yz_peer(o)
        pl.semaphore_signal(sem, inc=1, device_id=(x * 2 + yh, zz * 4 + yl * 2 + c), device_id_type=MESH)

    @pl.loop(1, 16)
    def _(o):
        rr = lax.rem(r + o // 2, 8)
        cc = lax.rem(c + lax.rem(o, 2), 2)
        pl.semaphore_signal(sem, inc=1, device_id=(rr, p * 2 + cc), device_id_type=MESH)

    pl.semaphore_wait(sem, 46)
    sent = []

    def send(src, dst, to, s_sem, r_sem):
        copy = pltpu.make_async_remote_copy(
            src_ref=src, dst_ref=dst, send_sem=s_sem, recv_sem=r_sem, device_id=to, device_id_type=MESH
        )
        copy.start()
        sent.append(copy)
        return copy

    vy = {}

    def start_vy(slot, t):
        vy[slot] = send(
            dvr.at[aligned((t * 2 + 1 - y) * 256, 256), :], v_y.at[slot], yn, vy_s.at[slot], vy_r.at[slot]
        )

    start_vy(4, mod8(z + 4))
    kz = {}
    t4 = mod8(z + 4)
    kz[0, 1] = send(dkr.at[aligned(t4 * 512, 256), :], k_in.at[0, 0, 0:256], zr, kz_s.at[0], kz_r.at[0])
    kz[1, 1] = send(
        dkr.at[aligned(t4 * 512 + 256, 256), :], k_in.at[1, 0, 256:512], zl, kz_s.at[4], kz_r.at[4]
    )
    xc = []
    for dx in range(1, 4):
        xx = lax.rem(x + dx, 4)
        for i, src in ((0, dkp), (1, dvp)):
            k = (dx - 1) * 2 + i
            xc.append(send(src.at[:, xx], x_in.at[dx - 1, i], (xx * 2 + y_hi, b), x_s.at[k], x_r.at[k]))
    for step in (3, 2, 1):
        start_vy(step, mod8(z + step))
        start_vy(8 - step, mod8(z - step))
    start_vy(0, z)
    mine_q = pltpu.make_async_copy(
        dq.at[aligned(c * 128, 128), :], gq.at[:, aligned(c * 896, 896)], q_sem.at[0]
    )
    mine_q.start()
    their_q = send(
        dq.at[aligned((1 - c) * 128, 128), :], gq.at[:, aligned(c * 896, 896)], sib, q_sem.at[1], q_sem.at[2]
    )

    def v_own(t, slot, lo, rows):
        own = dvr[aligned((t * 2 + y) * 256 + lo, rows), :].astype(f32)
        return own + v_y[slot, lo : lo + rows, :].astype(f32)

    vz = {}
    vy[4].wait_recv()
    for way, to in ((0, zr), (1, zl)):
        lo = way * 128
        v_out[way, 0, lo : lo + 128, :] = v_own(t4, 4, lo, 128).astype(bf16)
        vz[way, 1] = send(
            v_out.at[way, 0, lo : lo + 128], v_in.at[way, 0, lo : lo + 128], to,
            vz_s.at[way * 4], vz_r.at[way * 4],
        )
    for step in range(2, 5):
        for way, to in ((0, zr), (1, zl)):
            far = 5 - step
            t = mod8(z + far) if way == 0 else mod8(z - far)
            kz[way, step - 1].wait_recv()
            own = dkr[aligned(t * 512, 512), :]
            if step == 2:
                lo = way * 256
                other = 256 - lo
                k_out[way, 1, lo : lo + 256, :] = (
                    own[lo : lo + 256, :].astype(f32) + k_in[way, 0, lo : lo + 256, :].astype(f32)
                ).astype(bf16)
                k_out[way, 1, other : other + 256, :] = own[other : other + 256, :]
            else:
                k_out[way, step - 1] = (own.astype(f32) + k_in[way, step - 2].astype(f32)).astype(bf16)
            k = way * 4 + step - 1
            kz[way, step] = send(k_out.at[way, step - 1], k_in.at[way, step - 1], to, kz_s.at[k], kz_r.at[k])
        for way, to in ((0, zr), (1, zl)):
            far = 5 - step
            t = mod8(z + far) if way == 0 else mod8(z - far)
            slot = far if way == 0 else 8 - far
            vy[slot].wait_recv()
            vz[way, step - 1].wait_recv()
            if step == 2:
                lo = way * 128
                other = 128 - lo
                v_out[way, 1, lo : lo + 128, :] = (
                    v_own(t, slot, lo, 128) + v_in[way, 0, lo : lo + 128, :].astype(f32)
                ).astype(bf16)
                v_out[way, 1, other : other + 128, :] = v_own(t, slot, other, 128).astype(bf16)
            else:
                v_out[way, step - 1] = (v_own(t, slot, 0, 256) + v_in[way, step - 2].astype(f32)).astype(bf16)
            k = way * 4 + step - 1
            vz[way, step] = send(v_out.at[way, step - 1], v_in.at[way, step - 1], to, vz_s.at[k], vz_r.at[k])
        if step == 2:
            for copy in xc:
                copy.wait_recv()
            for i, src in ((0, dkp), (1, dvp)):
                xs[i] = (
                    src[:, x].astype(f32)
                    + x_in[0, i].astype(f32)
                    + x_in[1, i].astype(f32)
                    + x_in[2, i].astype(f32)
                ).astype(bf16)

            def yz_copy(o):
                yh, zz, yl = yz_peer(o)
                return pltpu.make_async_remote_copy(
                    src_ref=xs.at[:, zz * 2 + yl, aligned(yh * 16, 16), :],
                    dst_ref=yz_in.at[o],
                    send_sem=yz_s.at[o],
                    recv_sem=yz_r.at[o],
                    device_id=(x * 2 + yh, zz * 4 + yl * 2 + c),
                    device_id_type=MESH,
                )

            @pl.loop(1, 32)
            def _(o):
                yz_copy(o).start()

    yz_in[0] = xs[:, p, aligned(y_hi * 16, 16), :]

    @pl.loop(1, 32)
    def _(o):
        yz_copy(o).wait()

    g_out[...] = jnp.sum(yz_in[...].astype(f32), axis=0).astype(bf16)
    core = r // 4
    part = lax.rem(r, 4)

    def g_copy(o, i, out):
        rr = lax.rem(r + o, 8)
        return (
            g_out.at[i],
            out.at[aligned(part * 16, 16), aligned(c * 128, 128)],
            g_s.at[i * 8 + o],
            g_r.at[i * 8 + part * 2 + c],
            (rr, p * 2 + core),
        )

    for i, out in ((0, pkg), (1, pvg)):
        for o in range(8):
            src, dst, s_sem, r_sem, to = g_copy(o, i, out)
            if o == 0:

                @pl.when(core == c)
                def _():
                    pltpu.make_async_copy(src, dst, r_sem).start()

                @pl.when(core != c)
                def _():
                    pltpu.make_async_remote_copy(
                        src_ref=src, dst_ref=dst, send_sem=s_sem, recv_sem=r_sem, device_id=to, device_id_type=MESH
                    ).start()
            else:
                send(src, dst, to, s_sem, r_sem)

    for way in (0, 1):
        kz[way, 4].wait_recv()
    total = dkr[aligned(z * 512, 512), :].astype(f32) + k_in[0, 3].astype(f32) + k_in[1, 3].astype(f32)
    ky_out[...] = total.astype(bf16).reshape(2, 256, D)
    ky = send(ky_out.at[1 - y], ky_in, yn, ky_s, ky_r)
    vy[0].wait_recv()
    for way in (0, 1):
        vz[way, 4].wait_recv()
    fin[1] = (v_own(z, 0, 0, 256) + v_in[0, 3].astype(f32) + v_in[1, 3].astype(f32)).astype(bf16)
    ky.wait_recv()
    k_mine = (
        dkr[aligned((z * 2 + y) * 256, 256), :].astype(f32)
        + k_in[0, 3, aligned(y * 256, 256), :].astype(f32)
        + k_in[1, 3, aligned(y * 256, 256), :].astype(f32)
    )
    fin[0] = (k_mine + ky_in[...].astype(f32)).astype(bf16)
    last = []
    for i, out in ((0, gk), (1, gv)):
        mine = pltpu.make_async_copy(
            fin.at[i, aligned(c * 128, 128), :], out.at[:, aligned(c * 128, 128)], f_sem.at[i]
        )
        mine.start()
        theirs = send(
            fin.at[i, aligned((1 - c) * 128, 128), :], out.at[:, aligned(c * 128, 128)], sib,
            f_sem.at[2 + i], f_sem.at[4 + i],
        )
        last.append((mine, theirs))
    for mine, theirs in last:
        mine.wait()
        theirs.wait_recv()
    mine_q.wait()
    their_q.wait_recv()
    for i, out in ((0, pkg), (1, pvg)):
        for k in range(8):
            pltpu.make_async_copy(g_out.at[i], out.at[0:16, 0:128], g_r.at[i * 8 + k]).wait()

        @pl.when(core != c)
        def _():
            pltpu.make_async_copy(g_out.at[i], out.at[0:16, 0:128], g_s.at[i * 8]).wait()

    for copy in sent:
        copy.wait_send()


def shards(q, rk, rv, pk, pv, go, lengths):
    rows = q.shape[1]
    q, rk, rv, go = q[0], rk[0], rv[0], go[0]
    dma = pltpu.SemaphoreType.DMA

    def out(*shape):
        return jax.ShapeDtypeStruct(shape, bf16)

    qh, gh, kr, vr, kp, vp = pl.pallas_call(
        gather_kernel,
        out_shape=(
            out(2 * rows, 896), out(2 * rows, 896), out(RESP, D), out(RESP, D), out(PROMPT, D), out(PROMPT, D),
        ),
        in_specs=[ANY] * 6,
        out_specs=(ANY,) * 6,
        scratch_shapes=[
            dma((6,)), dma((6,)), dma((6,)), dma((2,)), dma((2,)),
            dma((16,)), dma((16,)), dma((16,)), dma((16,)), dma((16,)), dma((16,)),
        ],
        compiler_params=pltpu.CompilerParams(collective_id=0, has_side_effects=True),
        name="gather",
    )(q, go, rk, rv, pk, pv)

    n_keys = PROMPT + RESP
    dq, dkr, dvr, dkp, dvp = pl.pallas_call(
        compute_kernel,
        out_shape=(out(2 * rows, 896), out(RESP, D), out(RESP, D), out(PROMPT, D), out(PROMPT, D)),
        in_specs=[SMEM] + [VMEM] * 6,
        out_specs=(VMEM,) * 5,
        scratch_shapes=[
            pltpu.VMEM((256, 896), bf16),
            pltpu.VMEM((D, n_keys), bf16),
            pltpu.VMEM((D, 256), bf16),
            pltpu.VMEM((D, 256), bf16),
            pltpu.VMEM((n_keys, 256), bf16),
            pltpu.VMEM((n_keys, 256), f32),
            pltpu.VMEM((n_keys // KC, 8, 256), f32),
            pltpu.VMEM((n_keys, D), f32),
            pltpu.VMEM((n_keys, D), f32),
        ],
        compiler_params=pltpu.CompilerParams(vmem_limit_bytes=58 * 2**20),
        name="grads",
    )(lengths, qh, gh, kr, vr, kp, vp)

    v = pltpu.VMEM
    gq, gk, gv, pkg, pvg = pl.pallas_call(
        reduce_kernel,
        out_shape=(out(rows, 1792), out(rows, 256), out(rows, 256), out(64, 256), out(64, 256)),
        in_specs=[VMEM] * 5,
        out_specs=(VMEM,) * 5,
        scratch_shapes=[
            v((2, 4, 512, D), bf16), v((2, 4, 512, D), bf16), v((2, 4, 256, D), bf16), v((2, 4, 256, D), bf16),
            v((8, 256, D), bf16), v((2, 256, D), bf16), v((256, D), bf16), v((2, 256, D), bf16),
            v((3, 2, 16, 32, D), bf16), v((2, 16, 32, D), bf16), v((32, 2, 16, D), bf16), v((2, 16, D), bf16),
            dma((3,)), dma((8,)), dma((8,)), dma((8,)), dma((8,)), dma((8,)), dma((8,)), dma, dma,
            dma((6,)), dma((6,)), dma((6,)), dma((32,)), dma((32,)), dma((16,)), dma((16,)),
        ],
        compiler_params=pltpu.CompilerParams(
            collective_id=1, has_side_effects=True, vmem_limit_bytes=40 * 2**20
        ),
        name="reduce",
    )(dq, dkr, dvr, dkp.reshape(16, 4, 32, D), dvp.reshape(16, 4, 32, D))
    return gq[None], gk[None], gv[None], pkg, pvg


def solution(mesh):
    in_specs = (
        P("resp", "blk", None),
        P("resp", "blk", None),
        P("resp", "blk", None),
        P("blk", None),
        P("blk", None),
        P("resp", "blk", None),
        P("resp"),
    )
    out_specs = (
        P("resp", "blk", None),
        P("resp", "blk", None),
        P("resp", "blk", None),
        P("blk", None),
        P("blk", None),
    )
    return jax.shard_map(shards, mesh=mesh, in_specs=in_specs, out_specs=out_specs, check_vma=False)
```

time: 700 us -> 158 us (0.23)
  waiting for transfers between devices: 346 us -> 0 us
  blocking collectives: 198 us -> 0 us
  Pallas kernels: 0 us -> 148 us
  local copies, waits for them, and re-layouts: 66.1 us -> 8.81 us
  matrix products: 42.5 us -> 0 us
  other arithmetic: 25.7 us -> 0 us
  between operations: 14.9 us -> 1.3 us
    all_gather x4 -> x0, waiting for transfers between devices: 243 us -> none  [the longest x1 66.3 us: shards(): lax.all_gather(response_value[0], 'blk', axis=0, tiled=True)]
    psum x1 -> x0, blocking collectives: 198 us -> none  [shards(): lax.psum((prompt_key_grads, prompt_value_grads), ('resp', 'blk'))]
    pallas_call x0 -> x3, Pallas kernels: none -> 148 us  [the longest x1 81.7 us: shards(): pl.pallas_call(reduce_kernel, out_shape=(out(rows, 1792), out(rows, 256),...]
    reduce_scatter x2 -> x0, waiting for transfers between devices: 102 us -> none  [the longest x1 102 us: shards(): lax.psum_scatter(resp_kgrad, 'blk', scatter_dimension=0, tiled=True)]
    dot_general x35 -> x0, matrix products: 42.5 us -> none  [the longest x5 10.1 us: block_grads(): jnp.einsum('gjtk,kgd->tgjd', grad_logit, key_block, preferred_element_typ...]
    dynamic_update_slice x36 -> x0, local copies, waits for them, and re-layouts: 25.7 us -> none  [the longest x16 9.89 us: resp_grads(): lax.dynamic_update_slice_in_dim(value_sum, value_add, block_start, 0)]
    add x17 -> x0, other arithmetic: 17.7 us -> none  [the longest x8 17.7 us: resp_grads(): return (query_sum + query_add, key_sum, value_sum)]
    dynamic_slice x14 -> x0, local copies, waits for them, and re-layouts: 14.2 us -> none  [take(): lax.dynamic_slice_in_dim(source, block_start, block_length, 0)]
  transfers between devices with their start and end apart: 6 -> 0, of which waited for: 5 -> 0; matrix products, arithmetic and copies ran while one was open for 5% -> 0% of each run, Pallas kernels for 0% -> 0%
where the time goes in v1:
time: 158 us
  Pallas kernels  148 us (94%)
  local copies, waits for them, and re-layouts  8.81 us (6%)
    pallas_call x1, Pallas kernels, shards(): pl.pallas_call(reduce_kernel, out_shape=(out(rows, 1792), out(rows, 256),...  81.7 us
    pallas_call x1, Pallas kernels, shards(): pl.pallas_call(gather_kernel, out_shape=(out(2 * rows, 896), out(2 * rows...  37.9 us
    pallas_call x1, Pallas kernels, shards(): pl.pallas_call(compute_kernel, out_shape=(out(2 * rows, 896), out(RESP, D...  28.2 us
    unnamed x15, local copies, waits for them, and re-layouts  8.81 us

profile of v1, /device:TPU:1, one launch (start us, length us, event | category | flops | bytes accessed | tf_op | source)
XLA Modules:
  0.0 158.0 jit_solution(4399194724339755153)
XLA Ops:
  1.3 37.9 %gather.1 = (bf16[256,896]{1,0:T(8,128)(2,1)}, bf16[256,896]{1,0:T(8,128)(2,1)}, bf16[4096,128]{1,0:T(8,128)(2,1)}, bf16[4096,128]{1,0:T(8,128)(2,1)}, bf16[2048...) custom-call(bf16[128,1792]{1,0:T(8,128)(2,1)} %bitcast.14, bf16[128,1792]{1,0:T(8,128)(2,1)} %bitcast.15, ...), custom_call_target="tpu_custom_call" | custom-call | tf_op jit(solution)/shard_map/gather/pallas_call | solution.py:487
  39.2 28.2 %grads.1 = (bf16[256,896]{1,0:T(8,128)(2,1)}, bf16[4096,128]{1,0:T(8,128)(2,1)}, bf16[4096,128]{1,0:T(8,128)(2,1)}, bf16[2048,128]{1,0:T(8,128)(2,1)}, bf16[2048,128]{1,0:T(8,128)(2,1)}) custom-call(s32[1]{0:T(128)S(6)} %copy.17.length, bf16[256,896]{1,0:T(8,128)(2,1)} %get-tuple-element.21.q, bf16[256,896]{1,0:T(8,128)(2,1)} %get-tuple-element.22.g_in, ...), custom_call_target="tpu_custom_call" | custom-call | tf_op jit(solution)/shard_map/grads/pallas_call | solution.py:503
  67.5 0.0 copy-start
  67.5 1.2 copy-done
  68.7 0.0 copy-start.1
  68.7 1.2 copy-done.1
  69.9 0.0 copy-start.2
  69.9 1.0 copy-done.2
  71.0 0.0 copy-start.3
  71.0 1.0 copy-done.3
  72.0 0.0 copy-start.4
  72.0 1.0 copy-done.4
  73.0 81.7 %reduce.1 = (bf16[128,1792]{1,0:T(8,128)(2,1)S(1)}, bf16[128,256]{1,0:T(8,128)(2,1)S(1)}, bf16[128,256]{1,0:T(8,128)(2,1)S(1)}, bf16[64,256]{1,0:T(8,128)(2,1)S(1)}, bf16[64,256]{1,0:T(8,128)(2,1)S(1)}) custom-call(bf16[256,896]{1,0:T(8,128)(2,1)S(1)} %copy-done.4, bf16[4096,128]{1,0:T(8,128)(2,1)S(1)} %copy-done, bf16[4096,128]{1,0:T(8,128)(2,1)S(1)} %copy-done.1, ...), custom_call_target="tpu_custom_call" | custom-call | tf_op jit(solution)/shard_map/reduce/pallas_call | solution.py:524
  154.7 0.8 copy.18
  155.5 0.6 copy.19
  156.1 0.6 copy.20
  156.8 0.6 copy.21
  157.4 0.6 copy.22
Async XLA Ops:
  67.5 1.2 copy-start
  68.7 1.2 copy-start.1
  69.9 1.0 copy-start.2
  71.0 1.0 copy-start.3
  72.0 1.0 copy-start.4

commit v2 on v0

v2 whole, which is shorter than its diff:
```python
import functools

import jax
import jax.numpy as jnp
from jax import lax
from jax.experimental import pallas as pl
from jax.experimental.pallas import tpu as pltpu
from jax.sharding import PartitionSpec as P

HEADS = 7
D = 128
RESP = 4096
PROMPT = 2048
SCALE = D**-0.5
LOG2E = 1.4426950408889634
KC = 512
f32, bf16 = jnp.float32, jnp.bfloat16
MESH = pl.DeviceIdType.MESH
ANY = pl.BlockSpec(memory_space=pl.ANY)
VMEM = pl.BlockSpec(memory_space=pltpu.VMEM)
SMEM = pl.BlockSpec(memory_space=pltpu.SMEM)


def dot(a, b):
    return jnp.dot(a, b, preferred_element_type=f32)


def place():
    r, b = lax.axis_index("resp"), lax.axis_index("blk")
    z, y, c = b // 4, lax.rem(b // 2, 2), lax.rem(b, 2)
    return r, b, z, y, c


def aligned(start, size):
    return pl.ds(pl.multiple_of(start, size), size)


def mod8(value):
    return lax.rem(value + 16, 8)


class Remote:
    def __init__(self, parts):
        self.parts = parts

    def make(self):
        src, dst, to, s_sem, r_sem = self.parts()
        return pltpu.make_async_remote_copy(
            src_ref=src, dst_ref=dst, send_sem=s_sem, recv_sem=r_sem, device_id=to, device_id_type=MESH
        )

    def start(self):
        self.make().start()

    def wait_recv(self):
        self.make().wait_recv()

    def wait_send(self):
        self.make().wait_send()


def fused_kernel(
    length, q, g, rk, rv, pk, pv, gq, gk, gv, pkg, pvg,
    qh, gh, qt, gt, ks, vs, pb, db, mb, ms, ls, ds, cen, sb, sd, dqt, dqs,
    dkr, dvr, dkp, dvp, k_in, v_in, v_y, ky_out, ky_in, fin, x_in, xs, yz_in, g_out,
    own_sem, sib_s, sib_r, qg_own, qg_s, qg_r,
    ky_s, ky_r, kz_s, kz_r, vz_s, vz_r, vy_s, vy_r,
    rkz_s, rkz_r, rvz_s, rvz_r, rvy_s, rvy_r, rky_s, rky_r, f_sem,
    x_s, x_r, yz_s, yz_r, g_s, g_r, dq_own, dq_s, dq_r,
):
    r, b, z, y, c = place()
    x, y_hi = r // 2, lax.rem(r, 2)
    p = z * 2 + y
    sib = (r, b + 1 - 2 * c)
    yn = (r, b + 2 - 4 * y)
    zr = (r, lax.rem(b + 4, 32))
    zl = (r, lax.rem(b + 28, 32))
    ways = ((0, zr), (1, zl))

    def yz_peer(o):
        yh = lax.rem(y_hi + o // 16, 2)
        zz = lax.rem(z + lax.rem(o // 2, 8), 8)
        yl = lax.rem(y + lax.rem(o, 2), 2)
        return yh, zz, yl

    sem = pltpu.get_barrier_semaphore()

    @pl.loop(1, 32)
    def _(o):
        yh, zz, yl = yz_peer(o)
        pl.semaphore_signal(sem, inc=1, device_id=(x * 2 + yh, zz * 4 + yl * 2 + c), device_id_type=MESH)

    @pl.loop(1, 16)
    def _(o):
        rr = lax.rem(r + o // 2, 8)
        cc = lax.rem(c + lax.rem(o, 2), 2)
        pl.semaphore_signal(sem, inc=1, device_id=(rr, p * 2 + cc), device_id_type=MESH)

    pl.semaphore_wait(sem, 46)
    sent = {}

    def send(key, parts):
        copy = Remote(parts)
        copy.start()
        sent[key] = copy
        return copy

    def drain(pending):
        for copy in pending:
            copy.wait_recv()

    def swap(src, dst, width, mine_sem, s_sem, r_sem, h=0):
        w = width * D
        mine = pltpu.make_async_copy(src.at[:, aligned(c * w + h * D, D)], dst, mine_sem)
        mine.start()
        theirs = send(
            ("swap", len(sent)), lambda: (src.at[:, aligned((1 - c) * w + h * D, D)], dst, sib, s_sem, r_sem)
        )
        return mine, theirs

    first = PROMPT + p * 256 + c * 128
    swaps = []
    for i, (src, dst) in enumerate(
        (
            (pk, ks.at[aligned(p * 128 + c * 64, 64), :]),
            (pv, vs.at[aligned(p * 128 + c * 64, 64), :]),
            (rk, ks.at[aligned(first, 128), :]),
            (rv, vs.at[aligned(first, 128), :]),
        )
    ):
        swaps.append(swap(src, dst, 1, own_sem.at[i], sib_s.at[i], sib_r.at[i]))
    qg_swaps = []
    for i, (src, dst) in enumerate(((q, qh), (g, gh))):
        for h in range(HEADS):
            k = i * HEADS + h
            to = dst.at[h, aligned(c * 128, 128), :]
            qg_swaps.append(swap(src, to, HEADS, qg_own.at[k], qg_s.at[k], qg_r.at[k], h))
    for mine, theirs in swaps:
        mine.wait()
        theirs.wait_recv()

    def push(key, ref, span, to, s_sems, r_sems, k):
        def parts():
            part = ref.at[aligned(*span()), :]
            return part, part, to, s_sems.at[k], r_sems.at[k]

        return send(key, parts)

    base_of, rows_of = (0, PROMPT), (128, 256)
    pend = {}

    def start_ky(i):
        n = rows_of[i]
        pend["ky", i] = [
            push(("ky", i), ks, lambda: (base_of[i] + p * n, n), yn, ky_s, ky_r, i)
        ]

    def start_vz(i, step):
        n = rows_of[i]
        out = []
        for way, to in ways:

            def span(way=way):
                t = mod8(z - step + 1) if way == 0 else mod8(z + step - 1)
                start = base_of[i] + (t * 2 + y) * n
                return (start + way * (n // 2), n // 2) if step == 4 else (start, n)

            k = i * 8 + way * 4 + step - 1
            out.append(push(("vz", k), vs, span, to, vz_s, vz_r, k))
        pend["vz", i, step] = out

    def start_vy(i, slot):
        n = rows_of[i]
        k = i * 8 + slot

        def span():
            return base_of[i] + (mod8(z - slot) * 2 + y) * n, n

        pend["vy", i, slot] = [push(("vy", k), vs, span, yn, vy_s, vy_r, k)]

    def start_kz(i, step):
        n = rows_of[i]
        out = []
        for way, to in ways:

            def span(way=way):
                t = mod8(z - step + 1) if way == 0 else mod8(z + step - 1)
                start = base_of[i] + t * 2 * n
                return (start + way * n, n) if step == 4 else (start, 2 * n)

            k = i * 8 + way * 4 + step - 1
            out.append(push(("kz", k), ks, span, to, kz_s, kz_r, k))
        pend["kz", i, step] = out

    def ring(i, step):
        drain(pend["vz", i, step - 1])
        if step < 5:
            start_vz(i, step)
            start_vy(i, step - 1)
            start_vy(i, 9 - step)
        else:
            start_vy(i, 4)
        drain(pend["kz", i, step - 1])
        if step < 5:
            start_kz(i, step)

    start_ky(0)
    start_vz(0, 1)
    start_vy(0, 0)
    start_ky(1)
    start_vy(1, 0)
    drain(pend["ky", 0])
    start_kz(0, 1)

    dkr[...] = jnp.zeros_like(dkr)
    dvr[...] = jnp.zeros_like(dvr)
    dqt[...] = jnp.zeros_like(dqt)
    ms[...] = jnp.full_like(ms, -1e30)
    ls[...] = jnp.zeros_like(ls)
    ds[...] = jnp.zeros_like(ds)
    for mine, theirs in qg_swaps:
        mine.wait()
        theirs.wait_recv()
    live = lax.broadcasted_iota(jnp.int32, (256, D), 0) + p * 256 < length[0]
    for h in range(HEADS):
        gh[h] = jnp.where(live, gh[h].astype(f32), 0.0).astype(bf16)
        qt[h] = qh[h].T
        gt[h] = gh[h].T
    drain(pend["ky", 1])
    drain(pend["vy", 1, 0])
    own_rows = aligned(PROMPT + z * KC, KC)
    middle = jnp.mean(vs[own_rows, :].astype(f32), axis=0, keepdims=True)
    middle = jnp.broadcast_to(middle, (16, D)).astype(bf16)
    for h in range(HEADS):
        cen[h] = dot(middle, gt[h])[0:1]

    def stats(i, masked):
        rows = aligned(i * KC, KC)
        kc = ks[rows, :]
        vc = vs[rows, :]

        def logits(h):
            s = dot(kc, qt[h])
            if masked:
                key = lax.broadcasted_iota(jnp.int32, s.shape, 0)
                pos = lax.broadcasted_iota(jnp.int32, s.shape, 1) + y * 256
                s = jnp.where(key <= pos, s, -jnp.inf)
            sb[h % 2] = s
            return jnp.maximum(ms[h], jnp.max(s, axis=0, keepdims=True) * (SCALE * LOG2E))

        top = logits(0)
        for h in range(HEADS):
            ahead = logits(h + 1) if h + 1 < HEADS else None
            dp = dot(vc, gt[h]) - cen[h]
            back = jnp.exp2(ms[h] - top)
            w = jnp.exp2(sb[h % 2] * (SCALE * LOG2E) - top)
            ls[h] = ls[h] * back + jnp.sum(w, axis=0, keepdims=True)
            ds[h] = ds[h] * back + jnp.sum(w * dp, axis=0, keepdims=True)
            pb[h, rows, :] = w.astype(bf16)
            db[h, rows, :] = dp.astype(bf16)
            mb[i, h] = top
            ms[h] = top
            top = ahead

    stats(4 + z, True)
    ring(0, 2)
    ring(0, 3)
    start_vz(1, 1)
    start_kz(1, 1)
    ring(0, 4)
    ring(0, 5)
    for slot in range(8):
        drain(pend["vy", 0, slot])

    def vy_ready(*slots):
        for slot in slots:
            drain(pend["vy", 1, slot])

    stats_events = {
        2: (lambda: ring(1, 2),),
        4: (lambda: ring(1, 3), lambda: vy_ready(1, 7)),
        6: (lambda: ring(1, 4), lambda: vy_ready(2, 6)),
        8: (lambda: ring(1, 5), lambda: vy_ready(3, 5)),
        10: (lambda: vy_ready(4),),
    }

    def play(events, n):
        for k, acts in events.items():

            @pl.when(n == k)
            def _():
                for act in acts:
                    act()

    @pl.loop(0, 11)
    def _(n):
        play(stats_events, n)
        j = n - 4
        delta = jnp.where(lax.rem(n, 2) == 0, j // 2 + 1, 7 - j // 2)
        t = z - delta

        @pl.when((n < 4) | (t >= 0))
        def _():
            stats(jnp.where(n < 4, n, 4 + t), False)

    for h in range(HEADS):
        inv = 1.0 / ls[h]
        ls[h] = inv
        ds[h] = ds[h] * inv

    def grads(i):
        rows = aligned(i * KC, KC)
        kt = ks[rows, :].T
        dk = jnp.zeros((KC, D), f32)
        dv = jnp.zeros((KC, D), f32)
        for h in range(HEADS):
            w = pb[h, rows, :].astype(f32) * (jnp.exp2(mb[i, h] - ms[h]) * ls[h])
            d_logit = (w * (db[h, rows, :].astype(f32) - ds[h])).astype(bf16)
            sd[h] = d_logit
            dk = dk + dot(d_logit, qh[h])
            dv = dv + dot(w.astype(bf16), gh[h])
        for h in range(HEADS):
            dqt[h] += dot(kt, sd[h])
        return (dk * SCALE).astype(bf16), dv.astype(bf16)

    kz, vz, vy = {}, {}, {}
    xc = []

    def target(way, far):
        return mod8(z + far) if way == 0 else mod8(z - far)

    def send_vy(slot):
        def parts():
            return dvr.at[mod8(z + slot), 1 - y], v_y.at[slot], yn, rvy_s.at[slot], rvy_r.at[slot]

        vy[slot] = send(("rvy", slot), parts)

    def x_send():
        for dx in range(1, 4):
            for i, src in ((0, dkp), (1, dvp)):

                def parts(dx=dx, i=i, src=src):
                    k = (dx - 1) * 2 + i
                    xx = lax.rem(x + dx, 4)
                    return src.at[:, xx], x_in.at[dx - 1, i], (xx * 2 + y_hi, b), x_s.at[k], x_r.at[k]

                xc.append(send(("x", dx, i), parts))

    def add(ref, index, *terms):
        total = ref[index].astype(f32)
        for term in terms:
            total = total + term.astype(f32)
        ref[index] = total.astype(bf16)

    def k_step(step):
        for way, to in ways:
            t = target(way, 5 - step)
            half = pl.ds(way * 256, 256)

            def parts(way=way, to=to, half=half):
                t = target(way, 5 - step)
                k = way * 4 + step - 1
                src, dst = dkr.at[t], k_in.at[way, step - 1]
                if step == 1:
                    src, dst = dkr.at[t, half], k_in.at[way, 0, half]
                return src, dst, to, rkz_s.at[k], rkz_r.at[k]

            if step == 1:
                kz[way, 1] = send(("rkz", way, 1), parts)
                continue
            kz[way, step - 1].wait_recv()
            if step == 2:
                add(dkr, (t, half), k_in[way, 0, half])
            else:
                add(dkr, (t,), k_in[way, step - 2])
            kz[way, step] = send(("rkz", way, step), parts)

    def v_step(step):
        far = 5 - step
        if step == 1:
            vy[4].wait_recv()
            add(dvr, (mod8(z + 4), y), v_y[4])
        for way, to in ways:
            t = target(way, far)
            half = pl.ds(way * 128, 128)

            def parts(way=way, to=to, half=half):
                t = target(way, far)
                k = way * 4 + step - 1
                src, dst = dvr.at[t, y], v_in.at[way, step - 1]
                if step == 1:
                    src, dst = dvr.at[t, y, half], v_in.at[way, 0, half]
                return src, dst, to, rvz_s.at[k], rvz_r.at[k]

            if step == 1:
                vz[way, 1] = send(("rvz", way, 1), parts)
                continue
            slot = far if way == 0 else 8 - far
            vy[slot].wait_recv()
            vz[way, step - 1].wait_recv()
            if step == 2:
                add(dvr, (t, y), v_y[slot])
                add(dvr, (t, y, half), v_in[way, 0, half])
            else:
                add(dvr, (t, y), v_y[slot], v_in[way, step - 2])
            vz[way, step] = send(("rvz", way, step), parts)

    def yz_copy(o):
        yh, zz, yl = yz_peer(o)
        return pltpu.make_async_remote_copy(
            src_ref=xs.at[:, zz * 2 + yl, aligned(yh * 16, 16), :],
            dst_ref=yz_in.at[o],
            send_sem=yz_s.at[o],
            recv_sem=yz_r.at[o],
            device_id=(x * 2 + yh, zz * 4 + yl * 2 + c),
            device_id_type=MESH,
        )

    def yz_send():
        for copy in xc:
            copy.wait_recv()
        for i, src in ((0, dkp), (1, dvp)):
            xs[i] = (
                src[:, x].astype(f32) + x_in[0, i].astype(f32) + x_in[1, i].astype(f32) + x_in[2, i].astype(f32)
            ).astype(bf16)

        @pl.loop(1, 32)
        def _(o):
            yz_copy(o).start()

    def both(far):
        send_vy(far)
        send_vy(8 - far)

    grads_events = {
        4: (x_send,),
        5: (lambda: k_step(1), lambda: send_vy(4)),
        7: (lambda: both(3), lambda: k_step(2), lambda: v_step(1)),
        9: (lambda: both(2), lambda: k_step(3), lambda: v_step(2)),
        11: (lambda: both(1), lambda: k_step(4), lambda: v_step(3), yz_send),
    }

    @pl.loop(0, 12)
    def _(n):
        play(grads_events, n)
        j = n - 4
        far = 4 - (j + 1) // 2
        t = mod8(jnp.where(lax.rem(j + 8, 2) == 1, z + far, z - far))

        @pl.when((n < 4) | (t <= z))
        def _():
            dk, dv = grads(jnp.where(n < 4, n, 4 + t))

            @pl.when(n < 4)
            def _():
                dkp[pl.ds(n * 4, 4)] = dk.reshape(4, 4, 32, D)
                dvp[pl.ds(n * 4, 4)] = dv.reshape(4, 4, 32, D)

            @pl.when(n >= 4)
            def _():
                dkr[t] = dk
                dvr[t] = dv.reshape(2, 256, D)

    send_vy(0)
    v_step(4)

    dq_copies = []
    for h in range(HEADS):
        dqs[h] = (dqt[h].T * SCALE).astype(bf16)
        to = gq.at[:, aligned(c * 896 + h * D, D)]
        mine = pltpu.make_async_copy(dqs.at[h, aligned(c * 128, 128), :], to, dq_own.at[h])
        mine.start()
        theirs = send(
            ("dq", h),
            lambda h=h, to=to: (dqs.at[h, aligned((1 - c) * 128, 128), :], to, sib, dq_s.at[h], dq_r.at[h]),
        )
        dq_copies.append((mine, theirs))

    for way in (0, 1):
        kz[way, 4].wait_recv()
    total = dkr[z].astype(f32) + k_in[0, 3].astype(f32) + k_in[1, 3].astype(f32)
    ky_out[...] = total.astype(bf16).reshape(2, 256, D)
    ky = send(("rky",), lambda: (ky_out.at[1 - y], ky_in, yn, rky_s, rky_r))

    yz_in[0] = xs[:, p, aligned(y_hi * 16, 16), :]

    @pl.loop(1, 32)
    def _(o):
        yz_copy(o).wait()

    g_out[...] = jnp.sum(yz_in[...].astype(f32), axis=0).astype(bf16)
    core = r // 4
    part = lax.rem(r, 4)
    for i, out in ((0, pkg), (1, pvg)):
        for o in range(8):
            src = g_out.at[i]
            dst = out.at[aligned(part * 16, 16), aligned(c * 128, 128)]
            s_sem, r_sem = g_s.at[i * 8 + o], g_r.at[i * 8 + part * 2 + c]
            to = (lax.rem(r + o, 8), p * 2 + core)
            if o == 0:

                @pl.when(core == c)
                def _():
                    pltpu.make_async_copy(src, dst, r_sem).start()

                @pl.when(core != c)
                def _():
                    pltpu.make_async_remote_copy(
                        src_ref=src, dst_ref=dst, send_sem=s_sem, recv_sem=r_sem, device_id=to, device_id_type=MESH
                    ).start()
            else:
                send(("g", i, o), lambda a=(src, dst, to, s_sem, r_sem): a)

    vy[0].wait_recv()
    for way in (0, 1):
        vz[way, 4].wait_recv()
    fin[1] = (
        dvr[z, y].astype(f32) + v_y[0].astype(f32) + v_in[0, 3].astype(f32) + v_in[1, 3].astype(f32)
    ).astype(bf16)
    lines = aligned(y * 256, 256)
    ky.wait_recv()
    fin[0] = (
        dkr[z, lines].astype(f32) + k_in[0, 3, lines].astype(f32) + k_in[1, 3, lines].astype(f32)
        + ky_in[...].astype(f32)
    ).astype(bf16)
    last = []
    for i, out in ((0, gk), (1, gv)):
        to = out.at[:, aligned(c * 128, 128)]
        mine = pltpu.make_async_copy(fin.at[i, aligned(c * 128, 128), :], to, f_sem.at[i])
        mine.start()
        theirs = send(
            ("fin", i),
            lambda i=i, to=to: (fin.at[i, aligned((1 - c) * 128, 128), :], to, sib, f_sem.at[2 + i], f_sem.at[4 + i]),
        )
        last.append((mine, theirs))
    for mine, theirs in last + dq_copies:
        mine.wait()
        theirs.wait_recv()
    for i, out in ((0, pkg), (1, pvg)):
        for k in range(8):
            pltpu.make_async_copy(g_out.at[i], out.at[0:16, 0:128], g_r.at[i * 8 + k]).wait()

        @pl.when(core != c)
        def _():
            pltpu.make_async_copy(g_out.at[i], out.at[0:16, 0:128], g_s.at[i * 8]).wait()

    for copy in sent.values():
        copy.wait_send()


def shards(q, rk, rv, pk, pv, go, lengths):
    rows = q.shape[1]
    dma = pltpu.SemaphoreType.DMA
    n_keys = PROMPT + RESP

    def out(*shape):
        return jax.ShapeDtypeStruct(shape, bf16)

    def v(*shape, dtype=bf16):
        return pltpu.VMEM(shape, dtype)

    def w(*shape):
        return pltpu.VMEM(shape, f32)

    gq, gk, gv, pkg, pvg = pl.pallas_call(
        fused_kernel,
        out_shape=(out(rows, 1792), out(rows, 256), out(rows, 256), out(64, 256), out(64, 256)),
        in_specs=[SMEM] + [ANY] * 6,
        out_specs=(VMEM,) * 5,
        scratch_shapes=[
            v(HEADS, 256, D), v(HEADS, 256, D), v(HEADS, D, 256), v(HEADS, D, 256), v(n_keys, D), v(n_keys, D),
            v(HEADS, n_keys, 256), v(HEADS, n_keys, 256), w(n_keys // KC, HEADS, 1, 256),
            w(HEADS, 1, 256), w(HEADS, 1, 256), w(HEADS, 1, 256), w(HEADS, 1, 256),
            w(2, KC, 256), v(HEADS, KC, 256), w(HEADS, D, 256), v(HEADS, 256, D),
            v(8, 512, D), v(8, 2, 256, D), v(16, 4, 32, D), v(16, 4, 32, D),
            v(2, 4, 512, D), v(2, 4, 256, D), v(8, 256, D), v(2, 256, D), v(256, D), v(2, 256, D),
            v(3, 2, 16, 32, D), v(2, 16, 32, D), v(32, 2, 16, D), v(2, 16, D),
            dma((4,)), dma((4,)), dma((4,)), dma((14,)), dma((14,)), dma((14,)),
            dma((2,)), dma((2,)), dma((16,)), dma((16,)), dma((16,)), dma((16,)), dma((16,)), dma((16,)),
            dma((8,)), dma((8,)), dma((8,)), dma((8,)), dma((8,)), dma((8,)), dma, dma, dma((6,)),
            dma((6,)), dma((6,)), dma((32,)), dma((32,)), dma((16,)), dma((16,)), dma((7,)), dma((7,)), dma((7,)),
        ],
        compiler_params=pltpu.CompilerParams(
            collective_id=0, has_side_effects=True, vmem_limit_bytes=63 * 2**20
        ),
        name="fused",
    )(lengths, q[0], go[0], rk[0], rv[0], pk, pv)
    return gq[None], gk[None], gv[None], pkg, pvg


def solution(mesh):
    in_specs = (
        P("resp", "blk", None),
        P("resp", "blk", None),
        P("resp", "blk", None),
        P("blk", None),
        P("blk", None),
        P("resp", "blk", None),
        P("resp"),
    )
    out_specs = (
        P("resp", "blk", None),
        P("resp", "blk", None),
        P("resp", "blk", None),
        P("blk", None),
        P("blk", None),
    )
    return jax.shard_map(shards, mesh=mesh, in_specs=in_specs, out_specs=out_specs, check_vma=False)
```

time: 700 us -> 109 us (0.16)
  waiting for transfers between devices: 346 us -> 0 us
  blocking collectives: 198 us -> 0 us
  Pallas kernels: 0 us -> 103 us
  local copies, waits for them, and re-layouts: 66.1 us -> 4.85 us
  matrix products: 42.5 us -> 0 us
  other arithmetic: 25.7 us -> 0 us
  between operations: 14.9 us -> 1.3 us
    all_gather x4 -> x0, waiting for transfers between devices: 243 us -> none  [the longest x1 66.3 us: shards(): lax.all_gather(response_value[0], 'blk', axis=0, tiled=True)]
    psum x1 -> x0, blocking collectives: 198 us -> none  [shards(): lax.psum((prompt_key_grads, prompt_value_grads), ('resp', 'blk'))]
    pallas_call x0 -> x1, Pallas kernels: none -> 103 us  [shards(): pl.pallas_call(fused_kernel, out_shape=(out(rows, 1792), out(rows, 256),...]
    reduce_scatter x2 -> x0, waiting for transfers between devices: 102 us -> none  [the longest x1 102 us: shards(): lax.psum_scatter(resp_kgrad, 'blk', scatter_dimension=0, tiled=True)]
    dot_general x35 -> x0, matrix products: 42.5 us -> none  [the longest x5 10.1 us: block_grads(): jnp.einsum('gjtk,kgd->tgjd', grad_logit, key_block, preferred_element_typ...]
    dynamic_update_slice x36 -> x0, local copies, waits for them, and re-layouts: 25.7 us -> none  [the longest x16 9.89 us: resp_grads(): lax.dynamic_update_slice_in_dim(value_sum, value_add, block_start, 0)]
    add x17 -> x0, other arithmetic: 17.7 us -> none  [the longest x8 17.7 us: resp_grads(): return (query_sum + query_add, key_sum, value_sum)]
    dynamic_slice x14 -> x0, local copies, waits for them, and re-layouts: 14.2 us -> none  [take(): lax.dynamic_slice_in_dim(source, block_start, block_length, 0)]
  transfers between devices with their start and end apart: 6 -> 0, of which waited for: 5 -> 0; matrix products, arithmetic and copies ran while one was open for 5% -> 0% of each run, Pallas kernels for 0% -> 0%
where the time goes in v2:
time: 109 us
  Pallas kernels  103 us (94%)
  local copies, waits for them, and re-layouts  4.85 us (4%)
  between operations  1.3 us (1%)
    pallas_call x1, Pallas kernels, shards(): pl.pallas_call(fused_kernel, out_shape=(out(rows, 1792), out(rows, 256),...  103 us
    unnamed x13, local copies, waits for them, and re-layouts  4.85 us

profile of v2, /device:TPU:1, one launch (start us, length us, event | category | flops | bytes accessed | tf_op | source)
XLA Modules:
  0.0 108.7 jit_solution(8490177542034261937)
XLA Ops:
  1.3 102.5 %fused.1 = (bf16[128,1792]{1,0:T(8,128)(2,1)}, bf16[128,256]{1,0:T(8,128)(2,1)}, bf16[128,256]{1,0:T(8,128)(2,1)}, bf16[64,256]{1,0:T(8,128)(2,1)}, bf16[64,256]{1,0:T(8,128)(2,1)}) custom-call(s32[1]{0:T(128)S(6)} %copy.17.length, bf16[128,1792]{1,0:T(8,128)(2,1)} %bitcast.8, bf16[128,1792]{1,0:T(8,128)(2,1)} %bitcast.9, bf16[128,256]{1,0:T(8,128)(2,1)} %bitcast.10, ...), custom_call_target="tpu_custom_call" | custom-call | tf_op jit(solution)/shard_map/fused/pallas_call | solution.py:565
  103.8 0.0 copy-start.1
  103.8 1.8 %copy.18 = bf16[1,128,1792]{2,1,0:T(8,128)(2,1)} copy(bf16[1,128,1792]{2,1,0:T(8,128)(2,1)} %bitcast.7) | data formatting | bytes 917504
  105.7 0.0 copy-done.1
  105.7 0.0 copy-start
  105.7 0.6 copy.19
  106.3 0.2 copy-done
  106.5 0.0 copy-start.3
  106.5 0.6 copy.20
  107.2 0.1 copy-done.3
  107.3 0.0 copy-start.2
  107.3 0.6 copy.21
  107.9 0.2 copy-done.2
  108.1 0.6 copy.22
Async XLA Ops:
  103.8 1.9 %copy-start.1 = (bf16[128,256]{1,0:T(8,128)(2,1)S(1)}, bf16[128,256]{1,0:T(8,128)(2,1)}, u32[]{:S(2)}) copy-start(bf16[128,256]{1,0:T(8,128)(2,1)} %get-tuple-element.11) | copy-start | bytes 196612
  105.7 0.9 copy-start
  106.5 0.8 copy-start.3
  107.3 0.8 copy-start.2

commit v3 on v2

--- a/solution.py
+++ b/solution.py
@@ -96,6 +96,49 @@
         cc = lax.rem(c + lax.rem(o, 2), 2)
         pl.semaphore_signal(sem, inc=1, device_id=(rr, p * 2 + cc), device_id_type=MESH)
 
+    first = PROMPT + p * 256 + c * 128
+    kv_parts = (
+        (pk, ks, p * 128 + c * 64, 64),
+        (pv, vs, p * 128 + c * 64, 64),
+        (rk, ks, first, 128),
+        (rv, vs, first, 128),
+    )
+    qg_parts = [(i, h) for i in range(2) for h in range(HEADS)]
+    own = []
+    for i, (src, dst, start, rows) in enumerate(kv_parts):
+        own.append(
+            pltpu.make_async_copy(src.at[:, aligned(c * D, D)], dst.at[aligned(start, rows), :], own_sem.at[i])
+        )
+    for i, h in qg_parts:
+        src, dst = ((q, qh), (g, gh))[i]
+        own.append(
+            pltpu.make_async_copy(
+                src.at[:, aligned(c * 896 + h * D, D)],
+                dst.at[h, aligned(c * 128, 128), :],
+                qg_own.at[i * HEADS + h],
+            )
+        )
+    for copy in own:
+        copy.start()
+    dkr[...] = jnp.zeros_like(dkr)
+    dvr[...] = jnp.zeros_like(dvr)
+    dqt[...] = jnp.zeros_like(dqt)
+    ms[...] = jnp.full_like(ms, -1e30)
+    ls[...] = jnp.zeros_like(ls)
+    ds[...] = jnp.zeros_like(ds)
+    for copy in own:
+        copy.wait()
+
+    def half_ready(half):
+        rows = aligned(half * 128, 128)
+        keep = lax.broadcasted_iota(jnp.int32, (128, D), 0) + (p * 256 + half * 128) < length[0]
+        for h in range(HEADS):
+            part = jnp.where(keep, gh[h, rows, :].astype(f32), 0.0).astype(bf16)
+            gh[h, rows, :] = part
+            gt[h, :, rows] = part.T
+            qt[h, :, rows] = qh[h, rows, :].T
+
+    half_ready(c)
     pl.semaphore_wait(sem, 46)
     sent = {}
 
@@ -109,35 +152,24 @@
         for copy in pending:
             copy.wait_recv()
 
-    def swap(src, dst, width, mine_sem, s_sem, r_sem, h=0):
-        w = width * D
-        mine = pltpu.make_async_copy(src.at[:, aligned(c * w + h * D, D)], dst, mine_sem)
-        mine.start()
-        theirs = send(
-            ("swap", len(sent)), lambda: (src.at[:, aligned((1 - c) * w + h * D, D)], dst, sib, s_sem, r_sem)
-        )
-        return mine, theirs
-
-    first = PROMPT + p * 256 + c * 128
-    swaps = []
-    for i, (src, dst) in enumerate(
-        (
-            (pk, ks.at[aligned(p * 128 + c * 64, 64), :]),
-            (pv, vs.at[aligned(p * 128 + c * 64, 64), :]),
-            (rk, ks.at[aligned(first, 128), :]),
-            (rv, vs.at[aligned(first, 128), :]),
-        )
-    ):
-        swaps.append(swap(src, dst, 1, own_sem.at[i], sib_s.at[i], sib_r.at[i]))
-    qg_swaps = []
-    for i, (src, dst) in enumerate(((q, qh), (g, gh))):
-        for h in range(HEADS):
+    swaps, qg_swaps = [], []
+    for i, (src, dst, start, rows) in enumerate(kv_parts):
+
+        def parts(i=i, src=src, dst=dst, start=start, rows=rows):
+            return src.at[:, aligned((1 - c) * D, D)], dst.at[aligned(start, rows), :], sib, sib_s.at[i], sib_r.at[i]
+
+        swaps.append(send(("kv", i), parts))
+    for i, h in qg_parts:
+
+        def parts(i=i, h=h):
+            src, dst = ((q, qh), (g, gh))[i]
             k = i * HEADS + h
-            to = dst.at[h, aligned(c * 128, 128), :]
-            qg_swaps.append(swap(src, to, HEADS, qg_own.at[k], qg_s.at[k], qg_r.at[k], h))
-    for mine, theirs in swaps:
-        mine.wait()
-        theirs.wait_recv()
+            col = aligned((1 - c) * 896 + h * D, D)
+            return src.at[:, col], dst.at[h, aligned(c * 128, 128), :], sib, qg_s.at[k], qg_r.at[k]
+
+        qg_swaps.append(send(("qg", i, h), parts))
+    for copy in swaps:
+        copy.wait_recv()
 
     def push(key, ref, span, to, s_sems, r_sems, k):
         def parts():
@@ -204,29 +236,16 @@
         if step < 5:
             start_kz(i, step)
 
-    start_ky(0)
-    start_vz(0, 1)
-    start_vy(0, 0)
-    start_ky(1)
-    start_vy(1, 0)
-    drain(pend["ky", 0])
-    start_kz(0, 1)
-
-    dkr[...] = jnp.zeros_like(dkr)
-    dvr[...] = jnp.zeros_like(dvr)
-    dqt[...] = jnp.zeros_like(dqt)
-    ms[...] = jnp.full_like(ms, -1e30)
-    ls[...] = jnp.zeros_like(ls)
-    ds[...] = jnp.zeros_like(ds)
-    for mine, theirs in qg_swaps:
-        mine.wait()
-        theirs.wait_recv()
-    live = lax.broadcasted_iota(jnp.int32, (256, D), 0) + p * 256 < length[0]
-    for h in range(HEADS):
-        gh[h] = jnp.where(live, gh[h].astype(f32), 0.0).astype(bf16)
-        qt[h] = qh[h].T
-        gt[h] = gh[h].T
-    drain(pend["ky", 1])
+    for i in (0, 1):
+        start_ky(i)
+        start_vz(i, 1)
+        start_vy(i, 0)
+    for i in (0, 1):
+        drain(pend["ky", i])
+        start_kz(i, 1)
+    for copy in qg_swaps:
+        copy.wait_recv()
+    half_ready(1 - c)
     drain(pend["vy", 1, 0])
     own_rows = aligned(PROMPT + z * KC, KC)
     middle = jnp.mean(vs[own_rows, :].astype(f32), axis=0, keepdims=True)
@@ -263,26 +282,32 @@
             top = ahead
 
     stats(4 + z, True)
+
+    def vy_ready(i, *slots):
+        for slot in slots:
+            drain(pend["vy", i, slot])
+
     ring(0, 2)
-    ring(0, 3)
-    start_vz(1, 1)
-    start_kz(1, 1)
-    ring(0, 4)
-    ring(0, 5)
-    for slot in range(8):
-        drain(pend["vy", 0, slot])
-
-    def vy_ready(*slots):
-        for slot in slots:
-            drain(pend["vy", 1, slot])
+    ring(1, 2)
 
     stats_events = {
-        2: (lambda: ring(1, 2),),
-        4: (lambda: ring(1, 3), lambda: vy_ready(1, 7)),
-        6: (lambda: ring(1, 4), lambda: vy_ready(2, 6)),
-        8: (lambda: ring(1, 5), lambda: vy_ready(3, 5)),
-        10: (lambda: vy_ready(4),),
+        0: (lambda: vy_ready(1, 1, 7),),
+        1: (lambda: ring(0, 3),),
+        2: (lambda: ring(0, 4), lambda: ring(1, 3), lambda: vy_ready(1, 2, 6)),
+        3: (lambda: ring(0, 5), lambda: vy_ready(0, *range(8))),
+        5: (lambda: ring(1, 4),),
+        7: (lambda: vy_ready(1, 3, 5),),
+        8: (lambda: ring(1, 5),),
+        10: (lambda: vy_ready(1, 4),),
     }
+    prompt_at = {3: 0, 5: 1, 6: 2, 8: 3}
+    back_at = {0: 1, 1: 7, 2: 2, 4: 6, 7: 3, 9: 5, 10: 4}
+
+    def lookup(table, n, other):
+        value = other
+        for k, v in table.items():
+            value = jnp.where(n == k, v, value)
+        return value
 
     def play(events, n):
         for k, acts in events.items():
@@ -295,13 +320,11 @@
     @pl.loop(0, 11)
     def _(n):
         play(stats_events, n)
-        j = n - 4
-        delta = jnp.where(lax.rem(n, 2) == 0, j // 2 + 1, 7 - j // 2)
-        t = z - delta
-
-        @pl.when((n < 4) | (t >= 0))
+        chunk = lookup(prompt_at, n, 4 + z - lookup(back_at, n, 0))
+
+        @pl.when((chunk >= 4) | (lookup(prompt_at, n, -1) >= 0))
         def _():
-            stats(jnp.where(n < 4, n, 4 + t), False)
+            stats(chunk, False)
 
     for h in range(HEADS):
         inv = 1.0 / ls[h]
@@ -476,12 +499,6 @@
         )
         dq_copies.append((mine, theirs))
 
-    for way in (0, 1):
-        kz[way, 4].wait_recv()
-    total = dkr[z].astype(f32) + k_in[0, 3].astype(f32) + k_in[1, 3].astype(f32)
-    ky_out[...] = total.astype(bf16).reshape(2, 256, D)
-    ky = send(("rky",), lambda: (ky_out.at[1 - y], ky_in, yn, rky_s, rky_r))
-
     yz_in[0] = xs[:, p, aligned(y_hi * 16, 16), :]
 
     @pl.loop(1, 32)
@@ -510,6 +527,12 @@
                     ).start()
             else:
                 send(("g", i, o), lambda a=(src, dst, to, s_sem, r_sem): a)
+
+    for way in (0, 1):
+        kz[way, 4].wait_recv()
+    total = dkr[z].astype(f32) + k_in[0, 3].astype(f32) + k_in[1, 3].astype(f32)
+    ky_out[...] = total.astype(bf16).reshape(2, 256, D)
+    ky = send(("rky",), lambda: (ky_out.at[1 - y], ky_in, yn, rky_s, rky_r))
 
     vy[0].wait_recv()
     for way in (0, 1):
@@ -548,6 +571,19 @@
         copy.wait_send()
 
 
+def hand_on_kernel(*refs):
+    ins, outs, held, sems = refs[:5], refs[5:10], refs[10:15], refs[15]
+    loads = [pltpu.make_async_copy(ins[i], held[i], sems.at[i]) for i in range(5)]
+    stores = [pltpu.make_async_copy(held[i], outs[i], sems.at[5 + i]) for i in range(5)]
+    for copy in loads:
+        copy.start()
+    for load, store in zip(loads, stores):
+        load.wait()
+        store.start()
+    for copy in stores:
+        copy.wait()
+
+
 def shards(q, rk, rv, pk, pv, go, lengths):
     rows = q.shape[1]
     dma = pltpu.SemaphoreType.DMA
@@ -562,11 +598,11 @@
     def w(*shape):
         return pltpu.VMEM(shape, f32)
 
-    gq, gk, gv, pkg, pvg = pl.pallas_call(
+    outs = pl.pallas_call(
         fused_kernel,
         out_shape=(out(rows, 1792), out(rows, 256), out(rows, 256), out(64, 256), out(64, 256)),
         in_specs=[SMEM] + [ANY] * 6,
-        out_specs=(VMEM,) * 5,
+        out_specs=(ANY,) * 5,
         scratch_shapes=[
             v(HEADS, 256, D), v(HEADS, 256, D), v(HEADS, D, 256), v(HEADS, D, 256), v(n_keys, D), v(n_keys, D),
             v(HEADS, n_keys, 256), v(HEADS, n_keys, 256), w(n_keys // KC, HEADS, 1, 256),
@@ -585,6 +621,15 @@
         ),
         name="fused",
     )(lengths, q[0], go[0], rk[0], rv[0], pk, pv)
+    gq, gk, gv, pkg, pvg = pl.pallas_call(
+        hand_on_kernel,
+        out_shape=tuple(jax.ShapeDtypeStruct(x.shape, x.dtype) for x in outs),
+        in_specs=[ANY] * 5,
+        out_specs=(ANY,) * 5,
+        scratch_shapes=[v(*x.shape) for x in outs] + [dma((10,))],
+        compiler_params=pltpu.CompilerParams(vmem_limit_bytes=63 * 2**20),
+        name="hand_on",
+    )(*outs)
     return gq[None], gk[None], gv[None], pkg, pvg
 
 

time: 109 us -> 99.7 us (0.915)
  local copies, waits for them, and re-layouts: 4.85 us -> 0 us
  Pallas kernels: 103 us -> 98.2 us
    pallas_call x1, Pallas kernels: 103 us -> 96.3 us  [shards(): pl.pallas_call(fused_kernel, out_shape=(out(rows, 1792), out(rows, 256),...]
    unnamed x13 -> x0, local copies, waits for them, and re-layouts: 4.85 us -> none
    pallas_call x0 -> x1, Pallas kernels: none -> 1.93 us  [shards(): pl.pallas_call(hand_on_kernel, out_shape=tuple((jax.ShapeDtypeStruct(x.sh...]
where the time goes in v3:
time: 99.7 us; the launch traced here: 99.5 us
  Pallas kernels  98.2 us (98%)
  between operations  1.29 us (1%)
    pallas_call x1, Pallas kernels, shards(): pl.pallas_call(fused_kernel, out_shape=(out(rows, 1792), out(rows, 256),...  96.3 us

profile of v3, /device:TPU:1, one launch (start us, length us, event | category | flops | bytes accessed | tf_op | source)
XLA Modules:
  0.0 99.5 jit_solution(17284808849963495872)
XLA Ops:
  1.3 96.3 %fused.1 = (bf16[128,1792]{1,0:T(8,128)(2,1)}, bf16[128,256]{1,0:T(8,128)(2,1)}, bf16[128,256]{1,0:T(8,128)(2,1)}, bf16[64,256]{1,0:T(8,128)(2,1)}, bf16[64,256]{1,0:T(8,128)(2,1)}) custom-call(s32[1]{0:T(128)S(6)} %copy.12.length, bf16[128,1792]{1,0:T(8,128)(2,1)} %bitcast.7, bf16[128,1792]{1,0:T(8,128)(2,1)} %bitcast.8, bf16[128,256]{1,0:T(8,128)(2,1)} %bitcast.9, ...), custom_call_target="tpu_custom_call" | custom-call | tf_op jit(solution)/shard_map/fused/pallas_call | solution.py:601
  97.6 1.9 %hand_on.1 = (bf16[128,1792]{1,0:T(8,128)(2,1)}, bf16[128,256]{1,0:T(8,128)(2,1)}, bf16[128,256]{1,0:T(8,128)(2,1)}, bf16[64,256]{1,0:T(8,128)(2,1)}, bf16[64,256]{1,0:T(8,128)(2,1)}) custom-call(bf16[128,1792]{1,0:T(8,128)(2,1)} %get-tuple-element.15.refs_0_, bf16[128,256]{1,0:T(8,128)(2,1)} %get-tuple-element.16.refs_1_, ...), custom_call_target="tpu_custom_call" | custom-call | tf_op jit(solution)/shard_map/hand_on/pallas_call | solution.py:624

commit v4 on v3

v4 whole, which is shorter than its diff:
```python
import functools

import jax
import jax.numpy as jnp
from jax import lax
from jax.experimental import pallas as pl
from jax.experimental.pallas import tpu as pltpu
from jax.sharding import PartitionSpec as P

HEADS = 7
D = 128
RESP = 4096
PROMPT = 2048
PBLOCKS = PROMPT // 128
SCALE = D**-0.5
LOG2E = 1.4426950408889634
KC = 512
f32, bf16 = jnp.float32, jnp.bfloat16
MESH = pl.DeviceIdType.MESH
ANY = pl.BlockSpec(memory_space=pl.ANY)
VMEM = pl.BlockSpec(memory_space=pltpu.VMEM)
SMEM = pl.BlockSpec(memory_space=pltpu.SMEM)


def dot(a, b):
    return jnp.dot(a, b, preferred_element_type=f32)


def place():
    r, b = lax.axis_index("resp"), lax.axis_index("blk")
    z, y, c = b // 4, lax.rem(b // 2, 2), lax.rem(b, 2)
    return r, b, z, y, c


def aligned(start, size):
    return pl.ds(pl.multiple_of(start, size), size)


def mod8(value):
    return lax.rem(value + 16, 8)


class Remote:
    def __init__(self, parts):
        self.parts = parts

    def make(self):
        src, dst, to, s_sem, r_sem = self.parts()
        return pltpu.make_async_remote_copy(
            src_ref=src, dst_ref=dst, send_sem=s_sem, recv_sem=r_sem, device_id=to, device_id_type=MESH
        )

    def start(self):
        self.make().start()

    def wait_recv(self):
        self.make().wait_recv()

    def wait_send(self):
        self.make().wait_send()


def fused_kernel(
    length, q, g, rk, rv, pk, pv, gq, gkv, pgkv,
    qh, gh, qt, gt, kv, shard, pb, db, mb, ms, ls, ds, cen, sb, sd, dqt, dqs,
    dkr, dvr, dp_kv, k_in, v_in, v_y, ky_out, ky_in, fin, x_in, xs, yz_in, g_out,
    own_sem, sib_s, sib_r, qg_own, qg_s, qg_r,
    ky_s, ky_r, rz_s, rz_r, vy_s, vy_r, pz_s, pz_r, px_s, px_r,
    rkz_s, rkz_r, rvz_s, rvz_r, rvy_s, rvy_r, rky_s, rky_r, f_sem,
    x_s, x_r, yz_s, yz_r, g_s, g_r, dq_own, dq_s, dq_r,
):
    r, b, z, y, c = place()
    x, y_hi = r // 2, lax.rem(r, 2)
    p = z * 2 + y
    ks, vs = kv.at[0], kv.at[1]
    sib = (r, b + 1 - 2 * c)
    yn = (r, b + 2 - 4 * y)
    zr = (r, lax.rem(b + 4, 32))
    zl = (r, lax.rem(b + 28, 32))
    ways = ((0, zr), (1, zl))

    def yz_peer(o):
        yh = lax.rem(y_hi + o // 16, 2)
        zz = lax.rem(z + lax.rem(o // 2, 8), 8)
        yl = lax.rem(y + lax.rem(o, 2), 2)
        return yh, zz, yl

    sem = pltpu.get_barrier_semaphore()

    @pl.loop(1, 32)
    def _(o):
        yh, zz, yl = yz_peer(o)
        pl.semaphore_signal(sem, inc=1, device_id=(x * 2 + yh, zz * 4 + yl * 2 + c), device_id_type=MESH)

    @pl.loop(1, 16)
    def _(o):
        rr = lax.rem(r + o // 2, 8)
        cc = lax.rem(c + lax.rem(o, 2), 2)
        pl.semaphore_signal(sem, inc=1, device_id=(rr, p * 2 + cc), device_id_type=MESH)

    kv_parts = (
        (pk, shard.at[0], lambda ref: ref.at[aligned(c * 2, 2)]),
        (pv, shard.at[1], lambda ref: ref.at[aligned(c * 2, 2)]),
        (rk, ks, lambda ref: ref.at[PBLOCKS + p * 2 + c]),
        (rv, vs, lambda ref: ref.at[PBLOCKS + p * 2 + c]),
    )
    qg_parts = [(i, h) for i in range(2) for h in range(HEADS)]
    own = []
    for i, (src, dst, part) in enumerate(kv_parts):
        own.append(pltpu.make_async_copy(src.at[:, :, aligned(c * D, D)], part(dst), own_sem.at[i]))
    for i, h in qg_parts:
        src, dst = ((q, qh), (g, gh))[i]
        own.append(
            pltpu.make_async_copy(
                src.at[:, aligned(c * 896 + h * D, D)],
                dst.at[h, aligned(c * 128, 128), :],
                qg_own.at[i * HEADS + h],
            )
        )
    for copy in own:
        copy.start()
    dkr[...] = jnp.zeros_like(dkr)
    dvr[...] = jnp.zeros_like(dvr)
    dqt[...] = jnp.zeros_like(dqt)
    ms[...] = jnp.full_like(ms, -1e30)
    ls[...] = jnp.zeros_like(ls)
    ds[...] = jnp.zeros_like(ds)
    for copy in own:
        copy.wait()

    def half_ready(half):
        rows = aligned(half * 128, 128)
        keep = lax.broadcasted_iota(jnp.int32, (128, D), 0) + (p * 256 + half * 128) < length[0]
        for h in range(HEADS):
            part = jnp.where(keep, gh[h, rows, :].astype(f32), 0.0).astype(bf16)
            gh[h, rows, :] = part
            gt[h, :, rows] = part.T
            qt[h, :, rows] = qh[h, rows, :].T

    half_ready(c)
    pl.semaphore_wait(sem, 46)
    sent = {}

    def send(key, parts):
        copy = Remote(parts)
        copy.start()
        sent[key] = copy
        return copy

    def drain(pending):
        for copy in pending:
            copy.wait_recv()

    swaps, qg_swaps = [], []
    for i, (src, dst, part) in enumerate(kv_parts):

        def parts(i=i, src=src, dst=dst, part=part):
            return src.at[:, :, aligned((1 - c) * D, D)], part(dst), sib, sib_s.at[i], sib_r.at[i]

        swaps.append(send(("kv", i), parts))
    for i, h in qg_parts:

        def parts(i=i, h=h):
            src, dst = ((q, qh), (g, gh))[i]
            k = i * HEADS + h
            col = aligned((1 - c) * 896 + h * D, D)
            return src.at[:, col], dst.at[h, aligned(c * 128, 128), :], sib, qg_s.at[k], qg_r.at[k]

        qg_swaps.append(send(("qg", i, h), parts))
    for copy in swaps:
        copy.wait_recv()
    kv[:, p, x] = shard[:, x]

    def zy_peer(o):
        return lax.rem(z + o // 2, 8), lax.rem(y + lax.rem(o, 2), 2)

    def piece_copy(o):
        zz, yl = zy_peer(o)
        return pltpu.make_async_remote_copy(
            src_ref=shard.at[:, x],
            dst_ref=kv.at[:, p, x],
            send_sem=pz_s.at[o],
            recv_sem=pz_r.at[o],
            device_id=(r, zz * 4 + yl * 2 + c),
            device_id_type=MESH,
        )

    streams = {"v": (0, vs, y), "k": (1, ks, y), "kb": (2, ks, 1 - y)}
    pend = {}

    def block(t, line):
        return PBLOCKS + (t * 2 + line) * 2

    def push(key, ref, span, to, s_sems, r_sems, k):
        def parts():
            start, size = span()
            part = ref.at[pl.ds(start, size)]
            return part, part, to, s_sems.at[k], r_sems.at[k]

        return send(key, parts)

    def start_z(name, step):
        number, ref, line = streams[name]
        out = []
        for way, to in ways:

            def span(way=way):
                t = mod8(z - step + 1) if way == 0 else mod8(z + step - 1)
                return (block(t, line) + way, 1) if step == 4 else (block(t, line), 2)

            k = number * 8 + way * 4 + step - 1
            out.append(push(("z", k), ref, span, to, rz_s, rz_r, k))
        pend[name, step] = out

    def start_vy(slot):
        def span():
            return block(mod8(z - slot), y), 2

        pend["vy", slot] = [push(("vy", slot), vs, span, yn, vy_s, vy_r, slot)]

    def ring(step):
        for name in ("v", "k", "kb"):
            drain(pend[name, step - 1])
            if step < 5:
                start_z(name, step)
            if name == "v":
                start_vy(step - 1)
                if step < 5:
                    start_vy(9 - step)

    pend["ky"] = [push(("ky",), ks, lambda: (block(z, y), 2), yn, ky_s, ky_r, 0)]
    start_z("v", 1)
    start_z("k", 1)
    start_vy(0)

    @pl.loop(1, 16)
    def _(o):
        piece_copy(o).start()

    drain(pend["ky"])
    start_z("kb", 1)
    for copy in qg_swaps:
        copy.wait_recv()
    half_ready(1 - c)
    drain(pend["vy", 0])
    middle = jnp.mean(vs[aligned(PBLOCKS + z * 4, 4)].reshape(KC, D).astype(f32), axis=0, keepdims=True)
    middle = jnp.broadcast_to(middle, (16, D)).astype(bf16)
    for h in range(HEADS):
        cen[h] = dot(middle, gt[h])[0:1]

    def stats(i, masked):
        rows = aligned(i * KC, KC)
        kc = ks[aligned(i * 4, 4)].reshape(KC, D)
        vc = vs[aligned(i * 4, 4)].reshape(KC, D)

        def logits(h):
            s = dot(kc, qt[h])
            if masked:
                key = lax.broadcasted_iota(jnp.int32, s.shape, 0)
                pos = lax.broadcasted_iota(jnp.int32, s.shape, 1) + y * 256
                s = jnp.where(key <= pos, s, -jnp.inf)
            sb[h % 2] = s
            return jnp.maximum(ms[h], jnp.max(s, axis=0, keepdims=True) * (SCALE * LOG2E))

        top = logits(0)
        for h in range(HEADS):
            ahead = logits(h + 1) if h + 1 < HEADS else None
            dp = dot(vc, gt[h]) - cen[h]
            back = jnp.exp2(ms[h] - top)
            w = jnp.exp2(sb[h % 2] * (SCALE * LOG2E) - top)
            ls[h] = ls[h] * back + jnp.sum(w, axis=0, keepdims=True)
            ds[h] = ds[h] * back + jnp.sum(w * dp, axis=0, keepdims=True)
            pb[h, rows, :] = w.astype(bf16)
            db[h, rows, :] = dp.astype(bf16)
            mb[i, h] = top
            ms[h] = top
            top = ahead

    stats(4 + z, True)

    def vy_ready(*slots):
        for slot in slots:
            drain(pend["vy", slot])

    ring(2)

    @pl.loop(1, 16)
    def _(o):
        piece_copy(o).wait()

    for half in range(2):
        pend["px", half] = []
        for dx in range(1, 4):

            def parts(half=half, dx=dx):
                k = half * 3 + dx - 1
                part = kv.at[:, pl.ds(half * 8, 8), x]
                return part, part, (lax.rem(x + dx, 4) * 2 + y_hi, b), px_s.at[k], px_r.at[k]

            pend["px", half].append(send(("px", half, dx), parts))

    stats_events = {
        0: (lambda: vy_ready(1, 7),),
        2: (lambda: ring(3), lambda: vy_ready(2, 6)),
        4: (lambda: ring(4), lambda: drain(pend["px", 0])),
        6: (lambda: vy_ready(3, 5),),
        8: (lambda: ring(5), lambda: vy_ready(4)),
        9: (lambda: drain(pend["px", 1]),),
    }
    prompt_at = {4: 0, 5: 1, 9: 2, 10: 3}
    back_at = {0: 1, 1: 7, 2: 2, 3: 6, 6: 3, 7: 5, 8: 4}

    def lookup(table, n, other):
        value = other
        for k, v in table.items():
            value = jnp.where(n == k, v, value)
        return value

    def play(events, n):
        for k, acts in events.items():

            @pl.when(n == k)
            def _():
                for act in acts:
                    act()

    @pl.loop(0, 11)
    def _(n):
        play(stats_events, n)
        chunk = lookup(prompt_at, n, 4 + z - lookup(back_at, n, 0))

        @pl.when((chunk >= 4) | (lookup(prompt_at, n, -1) >= 0))
        def _():
            stats(chunk, False)

    for h in range(HEADS):
        inv = 1.0 / ls[h]
        ls[h] = inv
        ds[h] = ds[h] * inv

    def grads(i):
        rows = aligned(i * KC, KC)
        kt = ks[aligned(i * 4, 4)].reshape(KC, D).T
        dk = jnp.zeros((KC, D), f32)
        dv = jnp.zeros((KC, D), f32)
        for h in range(HEADS):
            w = pb[h, rows, :].astype(f32) * (jnp.exp2(mb[i, h] - ms[h]) * ls[h])
            d_logit = (w * (db[h, rows, :].astype(f32) - ds[h])).astype(bf16)
            sd[h] = d_logit
            dk = dk + dot(d_logit, qh[h])
            dv = dv + dot(w.astype(bf16), gh[h])
        for h in range(HEADS):
            dqt[h] += dot(kt, sd[h])
        return (dk * SCALE).astype(bf16), dv.astype(bf16)

    kz, vz, vy = {}, {}, {}
    xc = []

    def target(way, far):
        return mod8(z + far) if way == 0 else mod8(z - far)

    def sends(way, step, zz):
        ahead = zz + 5 - step
        return (ahead >= 8) | (ahead <= 3) if way == 0 else zz >= 5 - step

    def receives(way, step):
        return sends(way, step, mod8(z - 1) if way == 0 else mod8(z + 1))

    def sees(slot):
        return mod8(z + slot) <= z

    def send_if(key, condition, parts):
        copy = Remote(parts)
        pl.when(condition())(copy.start)
        maybe_sent[key] = (condition, copy)
        return copy

    maybe_sent = {}

    def send_vy(slot):
        def parts():
            return dvr.at[mod8(z + slot), 1 - y], v_y.at[slot], yn, rvy_s.at[slot], rvy_r.at[slot]

        vy[slot] = send_if(("rvy", slot), lambda: sees(slot), parts)

    def wait_vy(slot, ref_index):
        @pl.when(sees(slot))
        def _():
            vy[slot].wait_recv()
            add(dvr, ref_index, v_y[slot])

    def x_send(half):
        for dx in range(1, 4):

            def parts(dx=dx):
                k = half * 3 + dx - 1
                span = pl.ds(half * 8, 8)
                xx = lax.rem(x + dx, 4)
                return dp_kv.at[:, span, xx], x_in.at[dx - 1, :, span], (xx * 2 + y_hi, b), x_s.at[k], x_r.at[k]

            xc.append(send(("x", half, dx), parts))

    def add(ref, index, *terms):
        total = ref[index].astype(f32)
        for term in terms:
            total = total + term.astype(f32)
        ref[index] = total.astype(bf16)

    k_lines = (1 - y, y)

    def k_step(step):
        for stream, line in enumerate(k_lines):
            for way, to in ways:
                t = target(way, 5 - step)
                half = pl.ds(way * 128, 128)

                def parts(stream=stream, line=line, way=way, to=to, half=half):
                    t = target(way, 5 - step)
                    k = stream * 8 + way * 4 + step - 1
                    src, dst = dkr.at[t, line], k_in.at[stream, way, step - 1]
                    if step == 1:
                        src, dst = dkr.at[t, line, half], k_in.at[stream, way, 0, half]
                    return src, dst, to, rkz_s.at[k], rkz_r.at[k]

                if step > 1:

                    @pl.when(receives(way, step - 1))
                    def _():
                        kz[stream, way, step - 1].wait_recv()
                        if step == 2:
                            add(dkr, (t, line, half), k_in[stream, way, 0, half])
                        else:
                            add(dkr, (t, line), k_in[stream, way, step - 2])

                kz[stream, way, step] = send_if(
                    ("rkz", stream, way, step), lambda way=way: sends(way, step, z), parts
                )

    def v_step(step):
        far = 5 - step
        if step == 1:
            wait_vy(4, (mod8(z + 4), y))
        for way, to in ways:
            t = target(way, far)
            half = pl.ds(way * 128, 128)

            def parts(way=way, to=to, half=half):
                t = target(way, far)
                k = way * 4 + step - 1
                src, dst = dvr.at[t, y], v_in.at[way, step - 1]
                if step == 1:
                    src, dst = dvr.at[t, y, half], v_in.at[way, 0, half]
                return src, dst, to, rvz_s.at[k], rvz_r.at[k]

            if step > 1:
                wait_vy(far if way == 0 else 8 - far, (t, y))

                @pl.when(receives(way, step - 1))
                def _():
                    vz[way, step - 1].wait_recv()
                    if step == 2:
                        add(dvr, (t, y, half), v_in[way, 0, half])
                    else:
                        add(dvr, (t, y), v_in[way, step - 2])

            vz[way, step] = send_if(("rvz", way, step), lambda way=way: sends(way, step, z), parts)

    def yz_copy(o):
        yh, zz, yl = yz_peer(o)
        return pltpu.make_async_remote_copy(
            src_ref=xs.at[:, zz * 2 + yl, aligned(yh * 16, 16), :],
            dst_ref=yz_in.at[o],
            send_sem=yz_s.at[o],
            recv_sem=yz_r.at[o],
            device_id=(x * 2 + yh, zz * 4 + yl * 2 + c),
            device_id_type=MESH,
        )

    def yz_send():
        for copy in xc:
            copy.wait_recv()
        for i in range(2):
            xs[i] = (
                dp_kv[i, :, x].astype(f32) + x_in[0, i].astype(f32) + x_in[1, i].astype(f32) + x_in[2, i].astype(f32)
            ).astype(bf16)

        @pl.loop(1, 32)
        def _(o):
            yz_copy(o).start()

    def both(far):
        send_vy(far)
        send_vy(8 - far)

    grads_events = {
        1: (lambda: k_step(1), lambda: send_vy(4)),
        3: (lambda: both(3),),
        4: (lambda: v_step(1),),
        5: (lambda: x_send(0), lambda: k_step(2)),
        7: (lambda: x_send(1), lambda: v_step(2)),
        9: (lambda: both(2), lambda: k_step(3)),
        11: (lambda: both(1),),
    }
    ahead_at = {0: 4, 1: 3, 2: 5, 7: 2, 8: 6, 9: 1, 10: 7, 11: 0}
    prompt_now = {3: 0, 4: 1, 5: 2, 6: 3}

    @pl.loop(0, 12)
    def _(n):
        play(grads_events, n)
        t = mod8(z + lookup(ahead_at, n, 0))
        is_prompt = (n >= 3) & (n <= 6)

        @pl.when(is_prompt | (t <= z))
        def _():
            chunk = lookup(prompt_now, n, 4 + t)
            dk, dv = grads(chunk)

            @pl.when(is_prompt)
            def _():
                dp_kv[0, pl.ds(chunk * 4, 4)] = dk.reshape(4, 4, 32, D)
                dp_kv[1, pl.ds(chunk * 4, 4)] = dv.reshape(4, 4, 32, D)

            @pl.when(jnp.logical_not(is_prompt))
            def _():
                dkr[t] = dk.reshape(2, 256, D)
                dvr[t] = dv.reshape(2, 256, D)

    send_vy(0)
    k_step(4)
    v_step(3)

    dq_copies = []
    for h in range(HEADS):
        dqs[h] = (dqt[h].T * SCALE).astype(bf16)
        to = gq.at[:, aligned(c * 896 + h * D, D)]
        mine = pltpu.make_async_copy(dqs.at[h, aligned(c * 128, 128), :], to, dq_own.at[h])
        mine.start()
        theirs = send(
            ("dq", h),
            lambda h=h, to=to: (dqs.at[h, aligned((1 - c) * 128, 128), :], to, sib, dq_s.at[h], dq_r.at[h]),
        )
        dq_copies.append((mine, theirs))
    yz_send()
    v_step(4)

    def last_terms(copies, ref, index, ins):
        for way in (0, 1):

            @pl.when(receives(way, 4))
            def _():
                copies(way).wait_recv()
                add(ref, index, ins(way))

    last_terms(lambda way: kz[0, way, 4], dkr, (z, 1 - y), lambda way: k_in[0, way, 3])
    ky_out[...] = dkr[z, 1 - y]
    ky = send(("rky",), lambda: (ky_out, ky_in, yn, rky_s, rky_r))

    yz_in[0] = xs[:, p, aligned(y_hi * 16, 16), :]

    @pl.loop(1, 32)
    def _(o):
        yz_copy(o).wait()

    g_out[...] = jnp.sum(yz_in[...].astype(f32), axis=0).astype(bf16)
    core = r // 4
    part = lax.rem(r, 4)
    for o in range(8):
        dst = pgkv.at[:, aligned(part * 16, 16), aligned(c * 128, 128)]
        s_sem, r_sem = g_s.at[o], g_r.at[part * 2 + c]
        to = (lax.rem(r + o, 8), p * 2 + core)
        if o == 0:

            @pl.when(core == c)
            def _():
                pltpu.make_async_copy(g_out, dst, r_sem).start()

            @pl.when(core != c)
            def _():
                pltpu.make_async_remote_copy(
                    src_ref=g_out, dst_ref=dst, send_sem=s_sem, recv_sem=r_sem, device_id=to, device_id_type=MESH
                ).start()
        else:
            send(("g", o), lambda a=(g_out, dst, to, s_sem, r_sem): a)

    last = []

    def finish(i, out):
        to = out.at[:, aligned(c * 128, 128)]
        mine = pltpu.make_async_copy(fin.at[i, aligned(c * 128, 128), :], to, f_sem.at[i])
        mine.start()
        theirs = send(
            ("fin", i),
            lambda: (fin.at[i, aligned((1 - c) * 128, 128), :], to, sib, f_sem.at[2 + i], f_sem.at[4 + i]),
        )
        last.append((mine, theirs))

    wait_vy(0, (z, y))
    last_terms(lambda way: vz[way, 4], dvr, (z, y), lambda way: v_in[way, 3])
    fin[1] = dvr[z, y]
    finish(1, gkv.at[1])
    last_terms(lambda way: kz[1, way, 4], dkr, (z, y), lambda way: k_in[1, way, 3])
    ky.wait_recv()
    fin[0] = (dkr[z, y].astype(f32) + ky_in[...].astype(f32)).astype(bf16)
    finish(0, gkv.at[0])
    for mine, theirs in last + dq_copies:
        mine.wait()
        theirs.wait_recv()
    for k in range(8):
        pltpu.make_async_copy(g_out, pgkv.at[:, 0:16, 0:128], g_r.at[k]).wait()

    @pl.when(core != c)
    def _():
        pltpu.make_async_copy(g_out, pgkv.at[:, 0:16, 0:128], g_s.at[0]).wait()

    for copy in sent.values():
        copy.wait_send()
    for condition, copy in maybe_sent.values():
        pl.when(condition())(copy.wait_send)


def hand_on_kernel(gq, gkv, pgkv, out_q, out_k, out_v, out_pk, out_pv, *held_and_sems):
    held, sems = held_and_sems[:5], held_and_sems[5]
    ins = (gq, gkv.at[0], gkv.at[1], pgkv.at[0], pgkv.at[1])
    outs = (out_q, out_k, out_v, out_pk, out_pv)
    loads = [pltpu.make_async_copy(ins[i], held[i], sems.at[i]) for i in range(5)]
    stores = [pltpu.make_async_copy(held[i], outs[i], sems.at[5 + i]) for i in range(5)]
    for copy in loads:
        copy.start()
    for load, store in zip(loads, stores):
        load.wait()
        store.start()
    for copy in stores:
        copy.wait()


def shards(q, rk, rv, pk, pv, go, lengths):
    rows = q.shape[1]
    dma = pltpu.SemaphoreType.DMA
    n_keys = PROMPT + RESP

    def out(*shape):
        return jax.ShapeDtypeStruct(shape, bf16)

    def v(*shape, dtype=bf16):
        return pltpu.VMEM(shape, dtype)

    def w(*shape):
        return pltpu.VMEM(shape, f32)

    outs = pl.pallas_call(
        fused_kernel,
        out_shape=(out(rows, 1792), out(2, rows, 256), out(2, 64, 256)),
        in_specs=[SMEM] + [ANY] * 6,
        out_specs=(ANY,) * 3,
        scratch_shapes=[
            v(HEADS, 256, D), v(HEADS, 256, D), v(HEADS, D, 256), v(HEADS, D, 256),
            v(2, n_keys // 128, 4, 32, D), v(2, 4, 32, D),
            v(HEADS, n_keys, 256), v(HEADS, n_keys, 256), w(n_keys // KC, HEADS, 1, 256),
            w(HEADS, 1, 256), w(HEADS, 1, 256), w(HEADS, 1, 256), w(HEADS, 1, 256),
            w(2, KC, 256), v(HEADS, KC, 256), w(HEADS, D, 256), v(HEADS, 256, D),
            v(8, 2, 256, D), v(8, 2, 256, D), v(2, 16, 4, 32, D),
            v(2, 2, 4, 256, D), v(2, 4, 256, D), v(8, 256, D), v(256, D), v(256, D), v(2, 256, D),
            v(3, 2, 16, 32, D), v(2, 16, 32, D), v(32, 2, 16, D), v(2, 16, D),
            dma((4,)), dma((4,)), dma((4,)), dma((14,)), dma((14,)), dma((14,)),
            dma((1,)), dma((1,)), dma((24,)), dma((24,)), dma((8,)), dma((8,)),
            dma((16,)), dma((16,)), dma((6,)), dma((6,)),
            dma((16,)), dma((16,)), dma((8,)), dma((8,)), dma((8,)), dma((8,)), dma, dma, dma((6,)),
            dma((6,)), dma((6,)), dma((32,)), dma((32,)), dma((8,)), dma((8,)), dma((7,)), dma((7,)), dma((7,)),
        ],
        compiler_params=pltpu.CompilerParams(
            collective_id=0, has_side_effects=True, vmem_limit_bytes=63 * 2**20
        ),
        name="fused",
    )(
        lengths, q[0], go[0], rk[0].reshape(4, 32, 256), rv[0].reshape(4, 32, 256),
        pk.reshape(2, 32, 256), pv.reshape(2, 32, 256),
    )
    results = ((rows, 1792), (rows, 256), (rows, 256), (64, 256), (64, 256))
    gq, gk, gv, pkg, pvg = pl.pallas_call(
        hand_on_kernel,
        out_shape=tuple(out(*shape) for shape in results),
        in_specs=[ANY] * 3,
        out_specs=(ANY,) * 5,
        scratch_shapes=[v(*shape) for shape in results] + [dma((10,))],
        compiler_params=pltpu.CompilerParams(vmem_limit_bytes=63 * 2**20),
        name="hand_on",
    )(*outs)
    return gq[None], gk[None], gv[None], pkg, pvg


def solution(mesh):
    in_specs = (
        P("resp", "blk", None),
        P("resp", "blk", None),
        P("resp", "blk", None),
        P("blk", None),
        P("blk", None),
        P("resp", "blk", None),
        P("resp"),
    )
    out_specs = (
        P("resp", "blk", None),
        P("resp", "blk", None),
        P("resp", "blk", None),
        P("blk", None),
        P("blk", None),
    )
    return jax.shard_map(shards, mesh=mesh, in_specs=in_specs, out_specs=out_specs, check_vma=False)
```

time: 99.7 us -> 94.9 us (0.952)
  Pallas kernels: 98.2 us -> 93.4 us
    pallas_call x2, Pallas kernels: 98.2 us -> 93.4 us  [the longest x1 91.4 us: shards(): pl.pallas_call(fused_kernel, out_shape=(out(rows, 1792), out(2, rows, 256...]
where the time goes in v4:
time: 94.9 us; the launch traced here: 94.7 us
  Pallas kernels  93.4 us (98%)
  between operations  1.29 us (1%)
    pallas_call x1, Pallas kernels, shards(): pl.pallas_call(fused_kernel, out_shape=(out(rows, 1792), out(2, rows, 256...  91.4 us
    pallas_call x1, Pallas kernels, shards(): pl.pallas_call(hand_on_kernel, out_shape=tuple((out(*shape) for shape in...  1.93 us

profile of v4, /device:TPU:1, one launch (start us, length us, event | category | flops | bytes accessed | tf_op | source)
XLA Modules:
  0.0 94.7 jit_solution(4137254032945720271)
XLA Ops:
  1.3 91.4 %fused.1 = (bf16[128,1792]{1,0:T(8,128)(2,1)}, bf16[2,128,256]{2,1,0:T(8,128)(2,1)}, bf16[2,64,256]{2,1,0:T(8,128)(2,1)}) custom-call(s32[1]{0:T(128)S(6)} %copy.12.length, bf16[128,1792]{1,0:T(8,128)(2,1)} %bitcast.9, bf16[128,1792]{1,0:T(8,128)(2,1)} %bitcast.10, bf16[4,32,256]{2,1,0:T(8,128)(2,1)} %bitcast.11, bf16[4,32,256]{2,1,0:T(8,128)(2,1)} %bitcast.12, ...), custom_call_target="tpu_custom_call" | custom-call | tf_op jit(solution)/shard_map/fused/pallas_call | solution.py:650
  92.7 1.9 %hand_on.1 = (bf16[128,1792]{1,0:T(8,128)(2,1)}, bf16[128,256]{1,0:T(8,128)(2,1)}, bf16[128,256]{1,0:T(8,128)(2,1)}, bf16[64,256]{1,0:T(8,128)(2,1)}, bf16[64,256]{1,0:T(8,128)(2,1)}) custom-call(bf16[128,1792]{1,0:T(8,128)(2,1)} %get-tuple-element.13.gq, bf16[2,128,256]{2,1,0:T(8,128)(2,1)} %get-tuple-element.14.gkv, bf16[2,64,256]{2,1,0:T(8,128)(2,1)} %get-tuple-element.15.pgkv), custom_call_target="tpu_custom_call" | custom-call | tf_op jit(solution)/shard_map/hand_on/pallas_call | solution.py:679

commit v5 on v4

--- a/solution.py
+++ b/solution.py
@@ -147,9 +147,21 @@
         sent[key] = copy
         return copy
 
+    maybe_sent = {}
+
+    def send_if(key, condition, parts):
+        copy = Remote(parts)
+        pl.when(condition())(copy.start)
+        maybe_sent[key] = (condition, copy)
+        return copy
+
     def drain(pending):
         for copy in pending:
             copy.wait_recv()
+
+    def drain_if(pending):
+        for condition, copy in pending:
+            pl.when(condition())(copy.wait_recv)
 
     swaps, qg_swaps = [], []
     for i, (src, dst, part) in enumerate(kv_parts):
@@ -191,13 +203,21 @@
     def block(t, line):
         return PBLOCKS + (t * 2 + line) * 2
 
-    def push(key, ref, span, to, s_sems, r_sems, k):
+    def passes(way, step, zz):
+        if way == 0:
+            return (zz <= 6) & (zz - step + 1 >= 0)
+        return (zz + step - 1 >= 8) | (zz + step - 1 <= 3)
+
+    def arrives(way, step):
+        return passes(way, step, mod8(z - 1) if way == 0 else mod8(z + 1))
+
+    def push(key, condition, ref, span, to, s_sems, r_sems, k):
         def parts():
             start, size = span()
             part = ref.at[pl.ds(start, size)]
             return part, part, to, s_sems.at[k], r_sems.at[k]
 
-        return send(key, parts)
+        return send_if(key, condition, parts) if condition else send(key, parts)
 
     def start_z(name, step):
         number, ref, line = streams[name]
@@ -209,18 +229,22 @@
                 return (block(t, line) + way, 1) if step == 4 else (block(t, line), 2)
 
             k = number * 8 + way * 4 + step - 1
-            out.append(push(("z", k), ref, span, to, rz_s, rz_r, k))
+            copy = push(("z", k), lambda way=way: passes(way, step, z), ref, span, to, rz_s, rz_r, k)
+            out.append((lambda way=way: arrives(way, step), copy))
         pend[name, step] = out
 
     def start_vy(slot):
         def span():
             return block(mod8(z - slot), y), 2
 
-        pend["vy", slot] = [push(("vy", slot), vs, span, yn, vy_s, vy_r, slot)]
-
-    def ring(step):
-        for name in ("v", "k", "kb"):
-            drain(pend[name, step - 1])
+        def seen():
+            return z >= slot
+
+        pend["vy", slot] = [(seen, push(("vy", slot), seen, vs, span, yn, vy_s, vy_r, slot))]
+
+    def ring(step, names=("v", "k", "kb")):
+        for name in names:
+            drain_if(pend[name, step - 1])
             if step < 5:
                 start_z(name, step)
             if name == "v":
@@ -228,7 +252,7 @@
                 if step < 5:
                     start_vy(9 - step)
 
-    pend["ky"] = [push(("ky",), ks, lambda: (block(z, y), 2), yn, ky_s, ky_r, 0)]
+    pend["ky"] = [push(("ky",), None, ks, lambda: (block(z, y), 2), yn, ky_s, ky_r, 0)]
     start_z("v", 1)
     start_z("k", 1)
     start_vy(0)
@@ -242,7 +266,7 @@
     for copy in qg_swaps:
         copy.wait_recv()
     half_ready(1 - c)
-    drain(pend["vy", 0])
+    drain_if(pend["vy", 0])
     middle = jnp.mean(vs[aligned(PBLOCKS + z * 4, 4)].reshape(KC, D).astype(f32), axis=0, keepdims=True)
     middle = jnp.broadcast_to(middle, (16, D)).astype(bf16)
     for h in range(HEADS):
@@ -280,9 +304,9 @@
 
     def vy_ready(*slots):
         for slot in slots:
-            drain(pend["vy", slot])
-
-    ring(2)
+            drain_if(pend["vy", slot])
+
+    ring(2, ("v", "k"))
 
     @pl.loop(1, 16)
     def _(o):
@@ -299,16 +323,17 @@
 
             pend["px", half].append(send(("px", half, dx), parts))
 
+    ring(2, ("kb",))
     stats_events = {
         0: (lambda: vy_ready(1, 7),),
-        2: (lambda: ring(3), lambda: vy_ready(2, 6)),
-        4: (lambda: ring(4), lambda: drain(pend["px", 0])),
-        6: (lambda: vy_ready(3, 5),),
-        8: (lambda: ring(5), lambda: vy_ready(4)),
-        9: (lambda: drain(pend["px", 1]),),
+        2: (lambda: ring(3), lambda: drain(pend["px", 0])),
+        4: (lambda: vy_ready(2, 6),),
+        6: (lambda: ring(4), lambda: drain(pend["px", 1])),
+        8: (lambda: ring(5), lambda: vy_ready(3, 5)),
+        10: (lambda: vy_ready(4),),
     }
-    prompt_at = {4: 0, 5: 1, 9: 2, 10: 3}
-    back_at = {0: 1, 1: 7, 2: 2, 3: 6, 6: 3, 7: 5, 8: 4}
+    prompt_at = {2: 0, 3: 1, 6: 2, 7: 3}
+    back_at = {0: 1, 1: 7, 4: 2, 5: 6, 8: 3, 9: 5, 10: 4}
 
     def lookup(table, n, other):
         value = other
@@ -369,14 +394,6 @@
     def sees(slot):
         return mod8(z + slot) <= z
 
-    def send_if(key, condition, parts):
-        copy = Remote(parts)
-        pl.when(condition())(copy.start)
-        maybe_sent[key] = (condition, copy)
-        return copy
-
-    maybe_sent = {}
-
     def send_vy(slot):
         def parts():
             return dvr.at[mod8(z + slot), 1 - y], v_y.at[slot], yn, rvy_s.at[slot], rvy_r.at[slot]
@@ -494,21 +511,22 @@
 
     grads_events = {
         1: (lambda: k_step(1), lambda: send_vy(4)),
-        3: (lambda: both(3),),
+        3: (lambda: x_send(0),),
         4: (lambda: v_step(1),),
-        5: (lambda: x_send(0), lambda: k_step(2)),
-        7: (lambda: x_send(1), lambda: v_step(2)),
+        5: (lambda: both(3), lambda: k_step(2)),
+        7: (lambda: x_send(1),),
+        8: (lambda: v_step(2),),
         9: (lambda: both(2), lambda: k_step(3)),
-        11: (lambda: both(1),),
+        11: (lambda: both(1), lambda: v_step(3)),
     }
-    ahead_at = {0: 4, 1: 3, 2: 5, 7: 2, 8: 6, 9: 1, 10: 7, 11: 0}
-    prompt_now = {3: 0, 4: 1, 5: 2, 6: 3}
+    ahead_at = {0: 4, 3: 3, 4: 5, 7: 2, 8: 6, 9: 1, 10: 7, 11: 0}
+    prompt_now = {1: 0, 2: 1, 5: 2, 6: 3}
 
     @pl.loop(0, 12)
     def _(n):
         play(grads_events, n)
         t = mod8(z + lookup(ahead_at, n, 0))
-        is_prompt = (n >= 3) & (n <= 6)
+        is_prompt = lookup(prompt_now, n, -1) >= 0
 
         @pl.when(is_prompt | (t <= z))
         def _():
@@ -526,8 +544,6 @@
                 dvr[t] = dv.reshape(2, 256, D)
 
     send_vy(0)
-    k_step(4)
-    v_step(3)
 
     dq_copies = []
     for h in range(HEADS):
@@ -541,6 +557,7 @@
         )
         dq_copies.append((mine, theirs))
     yz_send()
+    k_step(4)
     v_step(4)
 
     def last_terms(copies, ref, index, ins):

time: 94.9 us -> 90.6 us (0.955)
  Pallas kernels: 93.4 us -> 89.1 us
    pallas_call x1, Pallas kernels: 91.4 us -> 87.2 us  [shards(): pl.pallas_call(fused_kernel, out_shape=(out(rows, 1792), out(2, rows, 256...]
where the time goes in v5:
time: 90.6 us; the launch traced here: 90.4 us
  Pallas kernels  89.1 us (98%)
  between operations  1.29 us (1%)
    pallas_call x1, Pallas kernels, shards(): pl.pallas_call(fused_kernel, out_shape=(out(rows, 1792), out(2, rows, 256...  87.2 us
    pallas_call x1, Pallas kernels, shards(): pl.pallas_call(hand_on_kernel, out_shape=tuple((out(*shape) for shape in...  1.93 us

profile of v5, /device:TPU:1, one launch (start us, length us, event | category | flops | bytes accessed | tf_op | source)
XLA Modules:
  0.0 90.4 jit_solution(860515570305929751)
XLA Ops:
  1.3 87.2 %fused.1 = (bf16[128,1792]{1,0:T(8,128)(2,1)}, bf16[2,128,256]{2,1,0:T(8,128)(2,1)}, bf16[2,64,256]{2,1,0:T(8,128)(2,1)}) custom-call(s32[1]{0:T(128)S(6)} %copy.12.length, bf16[128,1792]{1,0:T(8,128)(2,1)} %bitcast.9, bf16[128,1792]{1,0:T(8,128)(2,1)} %bitcast.10, bf16[4,32,256]{2,1,0:T(8,128)(2,1)} %bitcast.11, bf16[4,32,256]{2,1,0:T(8,128)(2,1)} %bitcast.12, ...), custom_call_target="tpu_custom_call" | custom-call | tf_op jit(solution)/shard_map/fused/pallas_call | solution.py:667
  88.5 1.9 %hand_on.1 = (bf16[128,1792]{1,0:T(8,128)(2,1)}, bf16[128,256]{1,0:T(8,128)(2,1)}, bf16[128,256]{1,0:T(8,128)(2,1)}, bf16[64,256]{1,0:T(8,128)(2,1)}, bf16[64,256]{1,0:T(8,128)(2,1)}) custom-call(bf16[128,1792]{1,0:T(8,128)(2,1)} %get-tuple-element.13.gq, bf16[2,128,256]{2,1,0:T(8,128)(2,1)} %get-tuple-element.14.gkv, bf16[2,64,256]{2,1,0:T(8,128)(2,1)} %get-tuple-element.15.pgkv), custom_call_target="tpu_custom_call" | custom-call | tf_op jit(solution)/shard_map/hand_on/pallas_call | solution.py:696

commit v6 on v5

--- a/solution.py
+++ b/solution.py
@@ -252,14 +252,14 @@
                 if step < 5:
                     start_vy(9 - step)
 
+    @pl.loop(1, 16)
+    def _(o):
+        piece_copy(o).start()
+
     pend["ky"] = [push(("ky",), None, ks, lambda: (block(z, y), 2), yn, ky_s, ky_r, 0)]
     start_z("v", 1)
     start_z("k", 1)
     start_vy(0)
-
-    @pl.loop(1, 16)
-    def _(o):
-        piece_copy(o).start()
 
     drain(pend["ky"])
     start_z("kb", 1)
@@ -326,10 +326,12 @@
     ring(2, ("kb",))
     stats_events = {
         0: (lambda: vy_ready(1, 7),),
-        2: (lambda: ring(3), lambda: drain(pend["px", 0])),
-        4: (lambda: vy_ready(2, 6),),
-        6: (lambda: ring(4), lambda: drain(pend["px", 1])),
-        8: (lambda: ring(5), lambda: vy_ready(3, 5)),
+        1: (lambda: ring(3),),
+        2: (lambda: drain(pend["px", 0]),),
+        4: (lambda: ring(4), lambda: vy_ready(2, 6)),
+        6: (lambda: drain(pend["px", 1]),),
+        7: (lambda: ring(5),),
+        8: (lambda: vy_ready(3, 5),),
         10: (lambda: vy_ready(4),),
     }
     prompt_at = {2: 0, 3: 1, 6: 2, 7: 3}
@@ -545,6 +547,10 @@
 
     send_vy(0)
 
+    yz_send()
+    k_step(4)
+    v_step(4)
+
     dq_copies = []
     for h in range(HEADS):
         dqs[h] = (dqt[h].T * SCALE).astype(bf16)
@@ -556,21 +562,6 @@
             lambda h=h, to=to: (dqs.at[h, aligned((1 - c) * 128, 128), :], to, sib, dq_s.at[h], dq_r.at[h]),
         )
         dq_copies.append((mine, theirs))
-    yz_send()
-    k_step(4)
-    v_step(4)
-
-    def last_terms(copies, ref, index, ins):
-        for way in (0, 1):
-
-            @pl.when(receives(way, 4))
-            def _():
-                copies(way).wait_recv()
-                add(ref, index, ins(way))
-
-    last_terms(lambda way: kz[0, way, 4], dkr, (z, 1 - y), lambda way: k_in[0, way, 3])
-    ky_out[...] = dkr[z, 1 - y]
-    ky = send(("rky",), lambda: (ky_out, ky_in, yn, rky_s, rky_r))
 
     yz_in[0] = xs[:, p, aligned(y_hi * 16, 16), :]
 
@@ -598,6 +589,18 @@
                 ).start()
         else:
             send(("g", o), lambda a=(g_out, dst, to, s_sem, r_sem): a)
+
+    def last_terms(copies, ref, index, ins):
+        for way in (0, 1):
+
+            @pl.when(receives(way, 4))
+            def _():
+                copies(way).wait_recv()
+                add(ref, index, ins(way))
+
+    last_terms(lambda way: kz[0, way, 4], dkr, (z, 1 - y), lambda way: k_in[0, way, 3])
+    ky_out[...] = dkr[z, 1 - y]
+    ky = send(("rky",), lambda: (ky_out, ky_in, yn, rky_s, rky_r))
 
     last = []
 

time: 90.6 us -> 88.7 us (0.979)
  Pallas kernels: 89.1 us -> 87.3 us
    pallas_call x1, Pallas kernels: 87.2 us -> 85.3 us  [shards(): pl.pallas_call(fused_kernel, out_shape=(out(rows, 1792), out(2, rows, 256...]
where the time goes in v6:
time: 88.7 us; the launch traced here: 88.5 us
  Pallas kernels  87.3 us (98%)
  between operations  1.29 us (1%)
    pallas_call x1, Pallas kernels, shards(): pl.pallas_call(fused_kernel, out_shape=(out(rows, 1792), out(2, rows, 256...  85.3 us
    pallas_call x1, Pallas kernels, shards(): pl.pallas_call(hand_on_kernel, out_shape=tuple((out(*shape) for shape in...  1.93 us

profile of v6, /device:TPU:1, one launch (start us, length us, event | category | flops | bytes accessed | tf_op | source)
XLA Modules:
  0.0 88.5 jit_solution(10230194004006331311)
XLA Ops:
  1.3 85.3 %fused.1 = (bf16[128,1792]{1,0:T(8,128)(2,1)}, bf16[2,128,256]{2,1,0:T(8,128)(2,1)}, bf16[2,64,256]{2,1,0:T(8,128)(2,1)}) custom-call(s32[1]{0:T(128)S(6)} %copy.12.length, bf16[128,1792]{1,0:T(8,128)(2,1)} %bitcast.9, bf16[128,1792]{1,0:T(8,128)(2,1)} %bitcast.10, bf16[4,32,256]{2,1,0:T(8,128)(2,1)} %bitcast.11, bf16[4,32,256]{2,1,0:T(8,128)(2,1)} %bitcast.12, ...), custom_call_target="tpu_custom_call" | custom-call | tf_op jit(solution)/shard_map/fused/pallas_call | solution.py:670
  86.6 1.9 %hand_on.1 = (bf16[128,1792]{1,0:T(8,128)(2,1)}, bf16[128,256]{1,0:T(8,128)(2,1)}, bf16[128,256]{1,0:T(8,128)(2,1)}, bf16[64,256]{1,0:T(8,128)(2,1)}, bf16[64,256]{1,0:T(8,128)(2,1)}) custom-call(bf16[128,1792]{1,0:T(8,128)(2,1)} %get-tuple-element.13.gq, bf16[2,128,256]{2,1,0:T(8,128)(2,1)} %get-tuple-element.14.gkv, bf16[2,64,256]{2,1,0:T(8,128)(2,1)} %get-tuple-element.15.pgkv), custom_call_target="tpu_custom_call" | custom-call | tf_op jit(solution)/shard_map/hand_on/pallas_call | solution.py:699

commit v7 on v6

--- a/solution.py
+++ b/solution.py
@@ -314,7 +314,7 @@
 
     for half in range(2):
         pend["px", half] = []
-        for dx in range(1, 4):
+        for dx in (2, 1, 3):
 
             def parts(half=half, dx=dx):
                 k = half * 3 + dx - 1
@@ -409,7 +409,7 @@
             add(dvr, ref_index, v_y[slot])
 
     def x_send(half):
-        for dx in range(1, 4):
+        for dx in (2, 1, 3):
 
             def parts(dx=dx):
                 k = half * 3 + dx - 1
@@ -505,7 +505,7 @@
 
         @pl.loop(1, 32)
         def _(o):
-            yz_copy(o).start()
+            yz_copy(1 + lax.rem(o + 6, 31)).start()
 
     def both(far):
         send_vy(far)

time: 88.7 us -> 88.6 us (level)
  no operation moved by 1% of the time
where the time goes in v7:
time: 88.6 us; the launch traced here: 88.4 us
  Pallas kernels  87.1 us (98%)
  between operations  1.29 us (1%)
    pallas_call x1, Pallas kernels, shards(): pl.pallas_call(fused_kernel, out_shape=(out(rows, 1792), out(2, rows, 256...  85.2 us
    pallas_call x1, Pallas kernels, shards(): pl.pallas_call(hand_on_kernel, out_shape=tuple((out(*shape) for shape in...  1.93 us

profile of v7, /device:TPU:1, one launch (start us, length us, event | category | flops | bytes accessed | tf_op | source)
XLA Modules:
  0.0 88.4 jit_solution(8056216363854499980)
XLA Ops:
  1.3 85.2 %fused.1 = (bf16[128,1792]{1,0:T(8,128)(2,1)}, bf16[2,128,256]{2,1,0:T(8,128)(2,1)}, bf16[2,64,256]{2,1,0:T(8,128)(2,1)}) custom-call(s32[1]{0:T(128)S(6)} %copy.12.length, bf16[128,1792]{1,0:T(8,128)(2,1)} %bitcast.9, bf16[128,1792]{1,0:T(8,128)(2,1)} %bitcast.10, bf16[4,32,256]{2,1,0:T(8,128)(2,1)} %bitcast.11, bf16[4,32,256]{2,1,0:T(8,128)(2,1)} %bitcast.12, ...), custom_call_target="tpu_custom_call" | custom-call | tf_op jit(solution)/shard_map/fused/pallas_call | solution.py:670
  86.5 1.9 %hand_on.1 = (bf16[128,1792]{1,0:T(8,128)(2,1)}, bf16[128,256]{1,0:T(8,128)(2,1)}, bf16[128,256]{1,0:T(8,128)(2,1)}, bf16[64,256]{1,0:T(8,128)(2,1)}, bf16[64,256]{1,0:T(8,128)(2,1)}) custom-call(bf16[128,1792]{1,0:T(8,128)(2,1)} %get-tuple-element.13.gq, bf16[2,128,256]{2,1,0:T(8,128)(2,1)} %get-tuple-element.14.gkv, bf16[2,64,256]{2,1,0:T(8,128)(2,1)} %get-tuple-element.15.pgkv), custom_call_target="tpu_custom_call" | custom-call | tf_op jit(solution)/shard_map/hand_on/pallas_call | solution.py:699
